TPU v7x, 256 devices: a whole 4x4x8 slice. The times are simulated.
256 devices in a mesh: gx: 8 (over x, core), gy: 32 (over z, y).
Axes of the slice: x: 4, y: 4, z: 8, core: 2. Of those that a mesh axis runs over, the one named last changes fastest.
Arguments:
- start: float32 [256, 1024, 128], P('gx', 'gy')
- velocity: float32 [3, 256, 1024, 128], P(None, 'gx', 'gy'), may hold values from -1 to 1
- prior: float32 [8, 256, 1024, 128], P(None, 'gx', 'gy')
- shifts: float32 [8], replicated, may hold values from 0.05 to 1.95, as said below
Outputs:
- basis_new: float32 [9, 256, 1024, 128], P(None, 'gx', 'gy')
- coeffs: float32 [17, 9], replicated
Inputs may be any that keep to these rules, and one draw needn't show every extreme that they name: Newton shifts, one in each of 8 spread places over the operator's real range, in an order drawn from the seed.
All inputs are finite; a program needn't handle non-finite values.
Results may differ from a plain program's by a relative error of at most 0.0003.
Values sent between devices are 32-bit elements; how exact they have to be, the bound alone decides.
No kernel may reach another device: no remote copies, remote signals or barrier semaphores. Data moves between devices by JAX's collectives and lax.ppermute only.
A program may use at most 64 MiB of HBM per device.

v0:
```python
import functools

import jax
import jax.numpy as jnp
import numpy as np
from jax import lax
from jax.experimental import pallas as pl
from jax.experimental.pallas import tpu as pltpu
from jax.sharding import PartitionSpec as P

STEPS = 8
PRIOR = 8
NEW = STEPS + 1
FIELDS = PRIOR + NEW
H = STEPS
DRIFT = 0.3
AXES = ("gx", "gy")

EARLY = [(i, j) for i in range(9) for j in range(i, 9)]
LATE = [(i, j) for i in range(9, 17) for j in range(i, 17)]
CROSS = [[(i, j) for i in range(9) for j in range(lo, lo + 4)] for lo in (9, 13)]
PAIRS = EARLY + LATE + CROSS[0] + CROSS[1]
SLOTS = 160


def pair_tables():
    first = np.zeros((128, 256), np.float32)
    second = np.zeros((128, 256), np.float32)
    for p, (i, j) in enumerate(PAIRS):
        first[i, p] = 0.5 if i == j else 1.0
        second[j, p] = 1.0
    return first, second


def products(load, pairs, groups):
    used = sorted({f for pair in pairs for f in pair})

    def body(g, totals):
        tile = {f: load(f, g) for f in used}
        return tuple(t + tile[i] * tile[j] for t, (i, j) in zip(totals, pairs))

    zero = jnp.zeros((8, 128), jnp.float32)
    return lax.fori_loop(0, groups, body, (zero,) * len(pairs), unroll=2)


def tile_of(ref, field, g, blocks):
    x, y = g // blocks, g % blocks
    rows = pl.ds(pl.multiple_of(y * 8, 8), 8)
    return ref[x, rows, :] if field is None else ref[field, x, rows, :]


def early_kernel(prior_ref, start_ref, out_ref):
    blocks = start_ref.shape[1] // 8
    groups = start_ref.shape[0] * blocks

    def load(f, g):
        return tile_of(prior_ref, f, g, blocks) if f < 8 else tile_of(start_ref, None, g, blocks)

    for p, total in enumerate(products(load, EARLY, groups)):
        out_ref[p] = total


def stencil_kernel(
    shifts_ref, sides_ref, start_ref, vel_ref, yl_ref, yh_ref, xl_ref, xh_ref, cl_ref, ch_ref, prior_ref, early_ref,
    basis_ref, sums_ref,
    fld, alt, down, pri, sta, acc, sems,
):
    wx, wy = sta.shape[0], sta.shape[1]
    ex, ey = wx + 2 * H, wy + 2 * H
    o = 2 * H
    mid_x, mid_y = pl.ds(H, wx), pl.ds(o, wy)
    low_y, high_y = pl.ds(H, H), pl.ds(o + wy, H)
    low_x, high_x = pl.ds(0, H), pl.ds(H + wx, H)
    copies = [
        (start_ref, fld.at[0, mid_x, mid_y]),
        (vel_ref, fld.at[pl.ds(1, 3), mid_x, mid_y]),
        (yl_ref, fld.at[:, mid_x, low_y]),
        (yh_ref, fld.at[:, mid_x, high_y]),
        (xl_ref, fld.at[:, low_x, mid_y]),
        (xh_ref, fld.at[:, high_x, mid_y]),
        (cl_ref.at[:, :, pl.ds(0, H)], fld.at[:, low_x, low_y]),
        (cl_ref.at[:, :, pl.ds(H, H)], fld.at[:, low_x, high_y]),
        (ch_ref.at[:, :, pl.ds(0, H)], fld.at[:, high_x, low_y]),
        (ch_ref.at[:, :, pl.ds(H, H)], fld.at[:, high_x, high_y]),
        (start_ref, sta),
        (prior_ref, pri),
    ]
    copies = [pltpu.make_async_copy(src, dst, sems.at[k]) for k, (src, dst) in enumerate(copies)]
    for c in copies:
        c.start()
    for c in copies[:10]:
        c.wait()

    x_low, x_high, y_low, y_high = (sides_ref[k] for k in range(4))
    lane = lax.broadcasted_iota(jnp.int32, (1, 1, 128), 2)
    not_last = jnp.where(lane < 127, 1.0, 0.0)
    not_first = jnp.where(lane > 0, 1.0, 0.0)
    sixth = 1.0 / 6.0

    def rows_of(step, x, n, x_side):
        src, dst = (fld.at[0], alt) if step % 2 == 0 else (alt, fld.at[0])
        last = step == STEPS - 1
        lo, size = (o, wy) if last else (H, ey)
        keep = 1.0 - shifts_ref[step]
        here, ys = pl.ds(x, n), pl.ds(lo, size)
        c = src[here, ys, :]
        e, w = src[pl.ds(x + 1, n), ys, :], src[pl.ds(x - 1, n), ys, :]
        u, d = src[here, pl.ds(lo + 1, size), :], src[here, pl.ds(lo - 1, size), :]
        if step == 0:
            a0, a1 = DRIFT * fld[1, here, ys, :], DRIFT * fld[2, here, ys, :]
            a2 = DRIFT * fld[3, here, ys, :]
            up, dn = (a2 - sixth) * not_last, (-a2 - sixth) * not_first
            fld[1, here, ys, :], fld[2, here, ys, :] = a0, a1
            fld[3, here, ys, :], down[here, ys, :] = up, dn
        else:
            a0, a1 = fld[1, here, ys, :], fld[2, here, ys, :]
            up, dn = fld[3, here, ys, :], down[here, ys, :]
        above = pltpu.roll(c, 127, 2)
        below = pltpu.roll(c, 1, 2)
        r = keep * c - sixth * ((e + w) + (u + d)) + a0 * (e - w) + a1 * (u - d) + (up * above + dn * below)
        if x_side is None:
            basis_ref[step, pl.ds(x - H, n), :, :] = r if last else r[:, H : H + wy]
        if last:
            return
        ml, mh = y_low, y_high
        middle = r[:, H : H + wy]
        if x_side is not None:
            ml, mh, middle = ml * x_side, mh * x_side, middle * x_side
        dst[here, low_y, :] = r[:, :H] * ml
        dst[here, mid_y, :] = middle
        dst[here, high_y, :] = r[:, H + wy :] * mh

    for step in range(STEPS):
        side = STEPS - 1 - step
        for k in range(side):
            rows_of(step, H - 1 - k, 1, x_low)
            rows_of(step, H + wx + k, 1, x_high)

        def some(i, carry, step=step):
            rows_of(step, H + i * 2, 2, None)
            return carry

        lax.fori_loop(0, wx // 2, some, 0)

    for c in copies[10:]:
        c.wait()
    blocks = wy // 8
    groups = wx * blocks

    def load(f, g):
        if f < 8:
            return tile_of(pri, f, g, blocks)
        return tile_of(sta, None, g, blocks) if f == 8 else tile_of(basis_ref, f - 9, g, blocks)

    n = len(EARLY)
    acc[0 : n * 8, :] = early_ref[...].reshape(n * 8, 128)
    for pairs in (LATE, *CROSS):
        for p, total in enumerate(products(load, pairs, groups)):
            acc[(n + p) * 8 : (n + p) * 8 + 8, :] = total
        n += len(pairs)
    acc[n * 8 :, :] = jnp.zeros((SLOTS * 8 - n * 8, 128), jnp.float32)
    by_lane = acc[pl.ds(0, SLOTS, stride=8), :]
    for s in range(1, 8):
        by_lane = by_lane + acc[pl.ds(s, SLOTS, stride=8), :]
    total = lax.dot_general(
        jnp.ones((8, 128), jnp.float32), by_lane, (((1,), (1,)), ((), ())),
        precision=lax.Precision.HIGHEST, preferred_element_type=jnp.float32,
    )
    second = jnp.concatenate([total[:, 128:], jnp.zeros((8, 256 - SLOTS), jnp.float32)], axis=1)
    even = lax.broadcasted_iota(jnp.int32, (8, 128), 0) % 2 == 0
    both = jnp.where(even, total[:, :128], second)
    for k in range(sums_ref.shape[0] // 8):
        sums_ref[k * 8 : k * 8 + 8, :] = both


def combine_kernel(
    count, chunks,
    sums_ref, first_ref, second_ref, start_hbm, basis_hbm, prior_hbm,
    new_hbm, coeffs_ref,
    bas, pri, new, spread, in_sems, out_sems,
):
    wx, wy = bas.shape[1], bas.shape[2]
    part = wx // chunks
    loads = []
    for k in range(chunks):
        xs = pl.ds(k * part, part)
        loads.append([
            pltpu.make_async_copy(start_hbm.at[xs], bas.at[0, xs], in_sems.at[k, 0]),
            pltpu.make_async_copy(basis_hbm.at[:, xs], bas.at[pl.ds(1, STEPS), xs], in_sems.at[k, 1]),
            pltpu.make_async_copy(prior_hbm.at[:, xs], pri.at[:, xs], in_sems.at[k, 2]),
        ])
    for group in loads:
        for c in group:
            c.start()

    total = sums_ref[0:8, :]
    for k in range(1, sums_ref.shape[0] // 8):
        total = total + sums_ref[k * 8 : k * 8 + 8, :]
    total = total + pltpu.roll(total, 4, 0)
    total = (total + pltpu.roll(total, 2, 0)) * (1.0 / count)
    flat = jnp.concatenate([total[0:1, :], total[1:2, :]], axis=1)
    contract = functools.partial(
        lax.dot_general, dimension_numbers=(((1,), (1,)), ((), ())),
        precision=lax.Precision.HIGHEST, preferred_element_type=jnp.float32,
    )
    first, second = first_ref[...], second_ref[...]
    full = contract(first[:24] * flat, second) + contract(second[:24] * flat, first)
    top, low = full[0:8, :], full[8:24, :]
    inner = 2.0 * top
    for k in range(PRIOR):
        inner = inner - top[:, k : k + 1] * top[k : k + 1, :]
    gram = low
    for k in range(PRIOR):
        gram = gram - low[:, k : k + 1] * inner[k : k + 1, :]
    lane = lax.broadcasted_iota(jnp.int32, (16, 128), 1)
    row = lax.broadcasted_iota(jnp.int32, (16, 128), 0)
    work = jnp.where(lane < NEW, pltpu.roll(gram, 128 - PRIOR, 1), 0.0)
    work = work + jnp.where(lane == row + 16, 1.0, 0.0)
    work = work + jnp.where((lane >= 32) & (lane < 32 + PRIOR), pltpu.roll(low, 32, 1), 0.0)
    for k in range(NEW):
        pivot = work[k : k + 1, k : k + 1]
        scaled = work[k : k + 1, :] / jnp.sqrt(pivot)
        column = work[:, k : k + 1] / pivot
        work = jnp.where(row > k, work - column * work[k : k + 1, :], jnp.where(row == k, scaled, work))
    coeffs_ref[0:PRIOR, :] = pltpu.roll(top, 128 - PRIOR, 1)[:, :NEW]
    coeffs_ref[PRIOR:FIELDS, :] = jnp.where(lane >= row, work, 0.0)[:NEW, :NEW]
    for i in range(FIELDS):
        at = 16 + i if i < NEW else 32 + i - NEW
        spread[i] = jnp.broadcast_to(work[:, at : at + 1], (16, 128))

    stores = []
    for k in range(chunks):
        for c in loads[k]:
            c.wait()

        def some(g, carry, k=k):
            x, y = k * part + g // (wy // 16), g % (wy // 16)
            ys = pl.ds(pl.multiple_of(y * 16, 16), 16)
            tiles = [bas[i, x, ys, :] for i in range(NEW)] + [pri[i, x, ys, :] for i in range(PRIOR)]
            for j in range(NEW):
                r = spread[0, j : j + 1, :] * tiles[0]
                for i in range(1, j + 1):
                    r = r + spread[i, j : j + 1, :] * tiles[i]
                for i in range(NEW, FIELDS):
                    r = r - spread[i, j : j + 1, :] * tiles[i]
                new[j, x, ys, :] = r
            return carry

        lax.fori_loop(0, part * (wy // 16), some, 0)
        xs = pl.ds(k * part, part)
        stores.append(pltpu.make_async_copy(new.at[:, xs], new_hbm.at[:, xs], out_sems.at[k]))
        stores[-1].start()
    for c in stores:
        c.wait()


def on_device(start, velocity, prior, shifts):
    wx, wy, wz = start.shape
    nx, ny = lax.axis_size("gx"), lax.axis_size("gy")
    devices = nx * ny
    ahead_x, ahead_y = ([(i, i + 1) for i in range(n - 1)] for n in (nx, ny))
    back_x, back_y = ([(i + 1, i) for i in range(n - 1)] for n in (nx, ny))

    def edge(at, dim):
        cut = [slice(None)] * 3
        cut[dim] = slice(at, at + H)
        return jnp.concatenate([start[tuple(cut)][None], velocity[(slice(None), *cut)]], axis=0)

    yl = lax.ppermute(edge(wy - H, 1), "gy", ahead_y)
    yh = lax.ppermute(edge(0, 1), "gy", back_y)
    xl = lax.ppermute(edge(wx - H, 0), "gx", ahead_x)
    xh = lax.ppermute(edge(0, 0), "gx", back_x)
    cl = lax.ppermute(jnp.concatenate([yl[:, wx - H :], yh[:, wx - H :]], axis=2), "gx", ahead_x)
    ch = lax.ppermute(jnp.concatenate([yl[:, :H], yh[:, :H]], axis=2), "gx", back_x)
    ix, iy = lax.axis_index("gx"), lax.axis_index("gy")
    sides = jnp.stack([ix > 0, ix < nx - 1, iy > 0, iy < ny - 1]).astype(jnp.float32)

    f32 = jnp.float32
    vmem = pl.BlockSpec(memory_space=pltpu.VMEM)
    smem = pl.BlockSpec(memory_space=pltpu.SMEM)
    hbm = pl.BlockSpec(memory_space=pl.ANY)
    limit = pltpu.CompilerParams(vmem_limit_bytes=48 * 1024 * 1024)
    early = pl.pallas_call(
        early_kernel,
        out_shape=jax.ShapeDtypeStruct((len(EARLY), 8, 128), f32),
        in_specs=[vmem, vmem],
        out_specs=vmem,
        compiler_params=limit,
        name="early",
    )(prior, start)
    ex, ey = wx + 2 * H, wy + 4 * H
    basis, sums = pl.pallas_call(
        stencil_kernel,
        out_shape=(
            jax.ShapeDtypeStruct((STEPS, wx, wy, wz), f32),
            jax.ShapeDtypeStruct((devices * 2, 128), f32),
        ),
        in_specs=[smem, smem] + [hbm] * 9 + [vmem],
        out_specs=(vmem, vmem),
        scratch_shapes=[
            pltpu.VMEM((4, ex, ey, wz), f32),
            pltpu.VMEM((ex, ey, wz), f32),
            pltpu.VMEM((ex, ey, wz), f32),
            pltpu.VMEM((PRIOR, wx, wy, wz), f32),
            pltpu.VMEM((wx, wy, wz), f32),
            pltpu.VMEM((SLOTS * 8, 128), f32),
            pltpu.SemaphoreType.DMA((12,)),
        ],
        compiler_params=limit,
        name="stencil",
    )(shifts, sides, start, velocity, yl, yh, xl, xh, cl, ch, prior, early)
    every = lax.all_to_all(sums, AXES, 0, 0, tiled=True)
    chunks = 4
    first, second = pair_tables()
    basis_new, coeffs = pl.pallas_call(
        functools.partial(combine_kernel, float(devices * wx * wy * wz), chunks),
        out_shape=(
            jax.ShapeDtypeStruct((NEW, wx, wy, wz), f32),
            jax.ShapeDtypeStruct((FIELDS, NEW), f32),
        ),
        in_specs=[vmem, vmem, vmem, hbm, hbm, hbm],
        out_specs=(hbm, vmem),
        scratch_shapes=[
            pltpu.VMEM((NEW, wx, wy, wz), f32),
            pltpu.VMEM((PRIOR, wx, wy, wz), f32),
            pltpu.VMEM((NEW, wx, wy, wz), f32),
            pltpu.VMEM((FIELDS, 16, 128), f32),
            pltpu.SemaphoreType.DMA((chunks, 3)),
            pltpu.SemaphoreType.DMA((chunks,)),
        ],
        compiler_params=limit,
        name="combine",
    )(every, jnp.asarray(first), jnp.asarray(second), start, basis, prior)
    return basis_new, coeffs


def solution(mesh):
    return jax.shard_map(
        on_device,
        mesh=mesh,
        in_specs=(P("gx", "gy", None), P(None, "gx", "gy", None), P(None, "gx", "gy", None), P()),
        out_specs=(P(None, "gx", "gy", None), P()),
        check_vma=False,
    )
```

profile of v0, /device:TPU:1, one launch (start us, length us, event | category | flops | bytes accessed | tf_op | source)
XLA Modules:
  0.0 102.3 jit_solution(11697864874215125613)
XLA Ops:
  0.6 0.0 copy-start.1
  0.6 0.0 copy-start.2
  0.7 1.1 %slice_bitcast_fusion.2 = (f32[1,32,8,128]{3,2,1,0:T(8,128)S(1)}, f32[1,32,8,128]{3,2,1,0:T(8,128)S(1)}) fusion(f32[32,32,128]{2,1,0:T(8,128)} %start_hbm.1), kind=kLoop, calls=%fused_computation.8 | loop fusion | bytes 524288 | tf_op jit(solution)/shard_map/broadcast_in_dim | solution.py:267
  1.8 1.2 %fusion.1 = (f32[3,32,8,128]{3,2,1,0:T(8,128)S(1)}, f32[3,32,8,128]{3,2,1,0:T(8,128)S(1)}) fusion(f32[3,32,32,128]{3,2,1,0:T(8,128)} %vel_ref.1), kind=kLoop, calls=%fused_computation.12 | loop fusion | bytes 1572864 | tf_op jit(solution)/shard_map/slice | solution.py:267
  3.0 4.1 %collective-permute-start = (f32[4,32,8,128]{3,2,1,0:T(8,128)S(1)}, f32[4,32,8,128]{3,2,1,0:T(8,128)S(1)}, u32[]{:S(2)}, u32[]{:S(2)}) collective-permute-start(f32[4,32,8,128]{3,2,1,0:T(8,128)S(1)} %pad_maximum_fusion), channel_id=1, source_target_pairs={{0,1},{1,2},{2,3},{3,4},{4,5},{5,6},{6,7},{7,8},{8,9},{9,10},{10,1... | collective-permute-start | bytes 1572872 | tf_op jit(solution)/shard_map/ppermute | solution.py:269
  7.1 1.3 %collective-permute-start.1 = (f32[4,32,8,128]{3,2,1,0:T(8,128)S(1)}, f32[4,32,8,128]{3,2,1,0:T(8,128)S(1)}, u32[]{:S(2)}, u32[]{:S(2)}) collective-permute-start(f32[4,32,8,128]{3,2,1,0:T(8,128)S(1)} %pad_maximum_fusion.1), channel_id=1, source_target_pairs={{1,0},{2,1},{3,2},{4,3},{5,4},{6,5},{7,6},{8,7},{9,8},{10,9},{11,1... | collective-permute-start | bytes 1572872 | tf_op jit(solution)/shard_map/ppermute | solution.py:270
  8.4 0.0 copy-done.2
  8.4 0.1 fusion
  8.5 0.0 copy-done.1
  8.6 0.8 pad_maximum_fusion.2
  9.4 4.1 %collective-permute-start.2 = (f32[4,8,32,128]{3,2,1,0:T(8,128)}, f32[4,8,32,128]{3,2,1,0:T(8,128)}, u32[]{:S(2)}, u32[]{:S(2)}) collective-permute-start(f32[4,8,32,128]{3,2,1,0:T(8,128)} %pad_maximum_fusion.2), channel_id=1, source_target_pairs={{0,32},{32,64},{64,96},{96,128},{128,160},{160,192},{192,224},{1,3... | collective-permute-start | bytes 1572872 | tf_op jit(solution)/shard_map/ppermute | solution.py:271
  13.5 0.9 pad_maximum_fusion.3
  14.3 1.9 %collective-permute-start.3 = (f32[4,8,32,128]{3,2,1,0:T(8,128)}, f32[4,8,32,128]{3,2,1,0:T(8,128)}, u32[]{:S(2)}, u32[]{:S(2)}) collective-permute-start(f32[4,8,32,128]{3,2,1,0:T(8,128)} %pad_maximum_fusion.3), channel_id=1, source_target_pairs={{32,0},{64,32},{96,64},{128,96},{160,128},{192,160},{224,192},{33,... | collective-permute-start | bytes 1572872 | tf_op jit(solution)/shard_map/ppermute | solution.py:272
  16.3 1.4 %collective-permute-done.yl_ref = f32[4,32,8,128]{3,2,1,0:T(8,128)S(1)} collective-permute-done((f32[4,32,8,128]{3,2,1,0:T(8,128)S(1)}, f32[4,32,8,128]{3,2,1,0:T(8,128)S(1)}, u32[]{:S(2)}, u32[]{:S(2)}) %collective-permute-start) | collective-permute-done | bytes 524320 | tf_op jit(solution)/shard_map/ppermute | solution.py:269
  17.6 3.8 %collective-permute-done.1.yh_ref = f32[4,32,8,128]{3,2,1,0:T(8,128)S(1)} collective-permute-done((f32[4,32,8,128]{3,2,1,0:T(8,128)S(1)}, f32[4,32,8,128]{3,2,1,0:T(8,128)S(1)}, u32[]{:S(2)}, u32[]{:S(2)}) %collective-permute-start.1) | collective-permute-done | bytes 524320 | tf_op jit(solution)/shard_map/ppermute | solution.py:270
  21.5 0.7 pad_maximum_fusion.4
  22.2 4.9 %collective-permute-start.4 = (f32[4,8,16,128]{3,2,1,0:T(8,128)}, f32[4,8,16,128]{3,2,1,0:T(8,128)S(1)}, u32[]{:S(2)}, u32[]{:S(2)}) collective-permute-start(f32[4,8,16,128]{3,2,1,0:T(8,128)} %pad_maximum_fusion.4), channel_id=1, source_target_pairs={{0,32},{32,64},{64,96},{96,128},{128,160},{160,192},{192,224},{1,3... | collective-permute-start | bytes 786440 | tf_op jit(solution)/shard_map/ppermute | solution.py:273
  27.1 0.7 pad_maximum_fusion.5
  27.8 1.9 %collective-permute-start.5 = (f32[4,8,16,128]{3,2,1,0:T(8,128)}, f32[4,8,16,128]{3,2,1,0:T(8,128)}, u32[]{:S(2)}, u32[]{:S(2)}) collective-permute-start(f32[4,8,16,128]{3,2,1,0:T(8,128)} %pad_maximum_fusion.5), channel_id=1, source_target_pairs={{32,0},{64,32},{96,64},{128,96},{160,128},{192,160},{224,192},{33,... | collective-permute-start | bytes 786440 | tf_op jit(solution)/shard_map/ppermute | solution.py:274
  29.8 0.0 copy-start
  29.8 2.2 %copy-done = f32[8,32,32,128]{3,2,1,0:T(8,128)S(1)} copy-done((f32[8,32,32,128]{3,2,1,0:T(8,128)S(1)}, f32[8,32,32,128]{3,2,1,0:T(8,128)}, u32[]{:S(2)}) %copy-start) | copy-done | bytes 4194328
  31.9 2.6 %early.1.early_ref = f32[45,8,128]{2,1,0:T(8,128)S(1)} custom-call(f32[8,32,32,128]{3,2,1,0:T(8,128)S(1)} %copy-done, f32[32,32,128]{2,1,0:T(8,128)S(1)} %copy-done.1), custom_call_target="tpu_custom_call" | custom-call | tf_op jit(solution)/shard_map/early/pallas_call | solution.py:283
  34.6 0.1 add_convert_fusion.sides_ref
  34.7 0.0 collective-permute-done.2.xl_ref
  34.7 0.0 collective-permute-done.3.xh_ref
  34.7 0.0 collective-permute-done.4.cl_ref
  34.7 1.1 %collective-permute-done.5.ch_ref = f32[4,8,16,128]{3,2,1,0:T(8,128)} collective-permute-done((f32[4,8,16,128]{3,2,1,0:T(8,128)}, f32[4,8,16,128]{3,2,1,0:T(8,128)}, u32[]{:S(2)}, u32[]{:S(2)}) %collective-permute-start.5) | collective-permute-done | bytes 262176 | tf_op jit(solution)/shard_map/ppermute | solution.py:274
  35.8 24.7 %stencil.1 = (f32[8,32,32,128]{3,2,1,0:T(8,128)}, f32[512,128]{1,0:T(8,128)S(1)}) custom-call(f32[8]{0:T(128)S(1)} %copy-done.6, f32[4]{0:T(128)S(1)} %add_convert_fusion.sides_ref, f32[32,32,128]{2,1,0:T(8,128)S(1)} %copy-done.1, f32[3,32,32,128]{3,2,1,0:T(8,128)S(1)} %copy-done.2, f32[4,32,8,128]{3,2,1,0:T(8,128)S(1)} %collective-permute-done.yl_ref, ...), custom_call_target="tpu_custom_call" | custom-call | tf_op jit(solution)/shard_map/stencil/pallas_call | solution.py:292
  60.5 30.5 %all_to_all.11 = f32[256,2,128]{2,1,0:T(2,128)S(1)} all-to-all(f32[256,2,128]{2,1,0:T(2,128)S(1)} %bitcast.15), channel_id=1, replica_groups=mesh['gx'=8,'gy'=32] {'gx','gy'}, dimensions={0} | all-to-all | bytes 524288 | tf_op jit(solution)/shard_map/all_to_all | solution.py:312
  91.0 2.2 %copy-done.3 = f32[8,32,32,128]{3,2,1,0:T(8,128)S(1)} copy-done((f32[8,32,32,128]{3,2,1,0:T(8,128)S(1)}, f32[8,32,32,128]{3,2,1,0:T(8,128)}, u32[]{:S(2)}) %copy-start.3) | copy-done | bytes 4194328
  93.1 8.5 %combine.1 = (f32[9,32,32,128]{3,2,1,0:T(8,128)}, f32[17,9]{1,0:T(8,128)S(1)}) custom-call(f32[512,128]{1,0:T(8,128)S(1)} %bitcast.14, f32[128,256]{1,0:T(8,128)S(1)} %copy-done.5, f32[128,256]{1,0:T(8,128)S(1)} %copy-done.4, f32[32,32,128]{2,1,0:T(8,128)S(1)} %copy-done.1, f32[8,32,32,128]{3,2,1,0:T(8,128)S(1)} %copy-done.3, f32[8,32,32,128]{3,2,1,0:T(8,128)} %prior_hbm.1), custom_call_target="tpu_custom_call" | custom-call | tf_op jit(solution)/shard_map/combine/pallas_call | solution.py:315
  101.6 0.7 copy.8
  (12 shorter events, 0.1 us)
Async XLA Ops:
  0.6 7.9 %copy-start.1 = (f32[32,32,128]{2,1,0:T(8,128)S(1)}, f32[32,32,128]{2,1,0:T(8,128)}, u32[]{:S(2)}) copy-start(f32[32,32,128]{2,1,0:T(8,128)} %start_hbm.1) | copy-start | bytes 1572868
  0.6 7.8 %copy-start.2 = (f32[3,32,32,128]{3,2,1,0:T(8,128)S(1)}, f32[3,32,32,128]{3,2,1,0:T(8,128)}, u32[]{:S(2)}) copy-start(f32[3,32,32,128]{3,2,1,0:T(8,128)} %vel_ref.1) | copy-start | bytes 4718596
  3.0 14.6 %collective-permute-start = (f32[4,32,8,128]{3,2,1,0:T(8,128)S(1)}, f32[4,32,8,128]{3,2,1,0:T(8,128)S(1)}, u32[]{:S(2)}, u32[]{:S(2)}) collective-permute-start(f32[4,32,8,128]{3,2,1,0:T(8,128)S(1)} %pad_maximum_fusion), channel_id=1, source_target_pairs={{0,1},{1,2},{2,3},{3,4},{4,5},{5,6},{6,7},{7,8},{8,9},{9,10},{10,1... | collective-permute-start | bytes 1572872 | tf_op jit(solution)/shard_map/ppermute | solution.py:269
  7.1 14.4 %collective-permute-start.1 = (f32[4,32,8,128]{3,2,1,0:T(8,128)S(1)}, f32[4,32,8,128]{3,2,1,0:T(8,128)S(1)}, u32[]{:S(2)}, u32[]{:S(2)}) collective-permute-start(f32[4,32,8,128]{3,2,1,0:T(8,128)S(1)} %pad_maximum_fusion.1), channel_id=1, source_target_pairs={{1,0},{2,1},{3,2},{4,3},{5,4},{6,5},{7,6},{8,7},{9,8},{10,9},{11,1... | collective-permute-start | bytes 1572872 | tf_op jit(solution)/shard_map/ppermute | solution.py:270
  9.4 26.4 %copy-start.6 = (f32[8]{0:T(128)S(1)}, f32[8]{0:T(128)}, u32[]{:S(2)}) copy-start(f32[8]{0:T(128)} %shifts_ref.1) | copy-start | bytes 100
  9.4 25.3 %collective-permute-start.2 = (f32[4,8,32,128]{3,2,1,0:T(8,128)}, f32[4,8,32,128]{3,2,1,0:T(8,128)}, u32[]{:S(2)}, u32[]{:S(2)}) collective-permute-start(f32[4,8,32,128]{3,2,1,0:T(8,128)} %pad_maximum_fusion.2), channel_id=1, source_target_pairs={{0,32},{32,64},{64,96},{96,128},{128,160},{160,192},{192,224},{1,3... | collective-permute-start | bytes 1572872 | tf_op jit(solution)/shard_map/ppermute | solution.py:271
  14.3 20.3 %collective-permute-start.3 = (f32[4,8,32,128]{3,2,1,0:T(8,128)}, f32[4,8,32,128]{3,2,1,0:T(8,128)}, u32[]{:S(2)}, u32[]{:S(2)}) collective-permute-start(f32[4,8,32,128]{3,2,1,0:T(8,128)} %pad_maximum_fusion.3), channel_id=1, source_target_pairs={{32,0},{64,32},{96,64},{128,96},{160,128},{192,160},{224,192},{33,... | collective-permute-start | bytes 1572872 | tf_op jit(solution)/shard_map/ppermute | solution.py:272
  22.2 12.4 %collective-permute-start.4 = (f32[4,8,16,128]{3,2,1,0:T(8,128)}, f32[4,8,16,128]{3,2,1,0:T(8,128)S(1)}, u32[]{:S(2)}, u32[]{:S(2)}) collective-permute-start(f32[4,8,16,128]{3,2,1,0:T(8,128)} %pad_maximum_fusion.4), channel_id=1, source_target_pairs={{0,32},{32,64},{64,96},{96,128},{128,160},{160,192},{192,224},{1,3... | collective-permute-start | bytes 786440 | tf_op jit(solution)/shard_map/ppermute | solution.py:273
  27.8 8.0 %collective-permute-start.5 = (f32[4,8,16,128]{3,2,1,0:T(8,128)}, f32[4,8,16,128]{3,2,1,0:T(8,128)}, u32[]{:S(2)}, u32[]{:S(2)}) collective-permute-start(f32[4,8,16,128]{3,2,1,0:T(8,128)} %pad_maximum_fusion.5), channel_id=1, source_target_pairs={{32,0},{64,32},{96,64},{128,96},{160,128},{192,160},{224,192},{33,... | collective-permute-start | bytes 786440 | tf_op jit(solution)/shard_map/ppermute | solution.py:274
  29.8 2.2 %copy-start = (f32[8,32,32,128]{3,2,1,0:T(8,128)S(1)}, f32[8,32,32,128]{3,2,1,0:T(8,128)}, u32[]{:S(2)}) copy-start(f32[8,32,32,128]{3,2,1,0:T(8,128)} %prior_hbm.1) | copy-start | bytes 12582916
  34.7 56.3 %copy-start.4 = (f32[128,256]{1,0:T(8,128)S(1)}, f32[128,256]{1,0:T(8,128)}, u32[]{:S(2)}) copy-start(f32[128,256]{1,0:T(8,128)} %constant.20.clone.second_ref) | copy-start | bytes 393220
  34.7 56.3 %copy-start.5 = (f32[128,256]{1,0:T(8,128)S(1)}, f32[128,256]{1,0:T(8,128)}, u32[]{:S(2)}) copy-start(f32[128,256]{1,0:T(8,128)} %constant.19.clone.first_ref) | copy-start | bytes 393220
  91.0 2.2 %copy-start.3 = (f32[8,32,32,128]{3,2,1,0:T(8,128)S(1)}, f32[8,32,32,128]{3,2,1,0:T(8,128)}, u32[]{:S(2)}) copy-start(f32[8,32,32,128]{3,2,1,0:T(8,128)} %get-tuple-element.5.basis_hbm) | copy-start | bytes 12582916
where the time goes:
time: 103 us; the launch traced here: 102 us
  Pallas kernels  35.8 us (35%)
  blocking collectives  30.5 us (30%)
  starting transfers between devices  18.1 us (18%)
  local copies, waits for them, and re-layouts  7.52 us (7%)
  waiting for transfers between devices  6.34 us (6%)
  other arithmetic  3.29 us (3%)
    all_to_all x1, blocking collectives, on_device(): every = lax.all_to_all(sums, AXES, 0, 0, tiled=True)  30.5 us
    pallas_call x1, Pallas kernels, on_device(): pl.pallas_call(stencil_kernel, out_shape=(jax.ShapeDtypeStruct((STEPS, wx...  24.7 us
    pallas_call x1, Pallas kernels, on_device(): pl.pallas_call(functools.partial(combine_kernel, float(devices * wx * wy...  8.47 us
    ppermute x1, starting transfers between devices, on_device(): lax.ppermute(jnp.concatenate([yl[:, wx - H:], yh[:, wx - H:]], axis=2), '...  4.86 us
    unnamed x14, local copies, waits for them, and re-layouts  4.39 us
    ppermute x1, starting transfers between devices, on_device(): xl = lax.ppermute(edge(wx - H, 0), 'gx', ahead_x)  4.08 us
    ppermute x1, starting transfers between devices, on_device(): yl = lax.ppermute(edge(wy - H, 1), 'gy', ahead_y)  4.06 us
    ppermute x1, waiting for transfers between devices, on_device(): yh = lax.ppermute(edge(0, 1), 'gy', back_y)  3.85 us
  transfers between devices with their start and end apart: 6, of which 3 were waited for; matrix products, arithmetic and copies ran while one was open for 3% of the time, Pallas kernels for 3%

commit v1 on v0

--- a/solution.py
+++ b/solution.py
@@ -32,15 +32,57 @@
     return first, second
 
 
-def products(load, pairs, groups):
+def corner_rows():
+    at, pieces = 0, []
+    for d in range(1, H):
+        for f in range(4):
+            pieces.append((at, d, f, H - d))
+            at += H - d
+    return pieces
+
+
+CORNER = 2 * sum(n for _, _, _, n in corner_rows())
+
+
+def pack_kernel(start_ref, vel_ref, y_first, y_last, x_first, x_last, sems):
+    wx, wy = start_ref.shape[0], start_ref.shape[1]
+    full = slice(None)
+    copies = []
+    for out, cut in (
+        (y_last, (full, pl.ds(wy - H, H))),
+        (y_first, (full, pl.ds(0, H))),
+        (x_last, (pl.ds(wx - H, H), full)),
+        (x_first, (pl.ds(0, H), full)),
+    ):
+        copies.append((start_ref.at[cut], out.at[0]))
+        copies.append((vel_ref.at[(full, *cut)], out.at[pl.ds(1, 3)]))
+    copies = [pltpu.make_async_copy(src, dst, sems.at[k]) for k, (src, dst) in enumerate(copies)]
+    for c in copies:
+        c.start()
+    for c in copies:
+        c.wait()
+
+
+def corner_kernel(xl_ref, xh_ref, up_ref, down_ref):
+    wy = xl_ref.shape[2]
+    for at, d, f, n in corner_rows():
+        up_ref[at : at + n, :] = xl_ref[f, H - d, wy - n :, :]
+        down_ref[at : at + n, :] = xl_ref[f, H - d, :n, :]
+        at += CORNER // 2
+        up_ref[at : at + n, :] = xh_ref[f, d - 1, wy - n :, :]
+        down_ref[at : at + n, :] = xh_ref[f, d - 1, :n, :]
+
+
+def products(load, pairs, groups, start=None):
     used = sorted({f for pair in pairs for f in pair})
 
     def body(g, totals):
         tile = {f: load(f, g) for f in used}
         return tuple(t + tile[i] * tile[j] for t, (i, j) in zip(totals, pairs))
 
-    zero = jnp.zeros((8, 128), jnp.float32)
-    return lax.fori_loop(0, groups, body, (zero,) * len(pairs), unroll=2)
+    if start is None:
+        start = (jnp.zeros((8, 128), jnp.float32),) * len(pairs)
+    return lax.fori_loop(0, groups, body, start, unroll=8)
 
 
 def tile_of(ref, field, g, blocks):
@@ -49,23 +91,40 @@
     return ref[x, rows, :] if field is None else ref[field, x, rows, :]
 
 
-def early_kernel(prior_ref, start_ref, out_ref):
-    blocks = start_ref.shape[1] // 8
-    groups = start_ref.shape[0] * blocks
-
-    def load(f, g):
-        return tile_of(prior_ref, f, g, blocks) if f < 8 else tile_of(start_ref, None, g, blocks)
-
-    for p, total in enumerate(products(load, EARLY, groups)):
+def early_kernel(prior_hbm, start_hbm, out_ref, prior_ref, start_ref, sems):
+    wx, blocks = start_ref.shape[0], start_ref.shape[1] // 8
+    parts = sems.shape[0]
+    part = wx // parts
+    copies = []
+    for k in range(parts):
+        xs = pl.ds(k * part, part)
+        copies.append([
+            pltpu.make_async_copy(prior_hbm.at[:, xs], prior_ref.at[:, xs], sems.at[k, 0]),
+            pltpu.make_async_copy(start_hbm.at[xs], start_ref.at[xs], sems.at[k, 1]),
+        ])
+        for c in copies[-1]:
+            c.start()
+
+    totals = None
+    for k in range(parts):
+        for c in copies[k]:
+            c.wait()
+
+        def load(f, g, k=k):
+            g = g + k * part * blocks
+            return tile_of(prior_ref, f, g, blocks) if f < 8 else tile_of(start_ref, None, g, blocks)
+
+        totals = products(load, EARLY, part * blocks, totals)
+    for p, total in enumerate(totals):
         out_ref[p] = total
 
 
 def stencil_kernel(
     shifts_ref, sides_ref, start_ref, vel_ref, yl_ref, yh_ref, xl_ref, xh_ref, cl_ref, ch_ref, prior_ref, early_ref,
     basis_ref, sums_ref,
-    fld, alt, down, pri, sta, acc, sems,
+    fld, alt, down, acc, sems,
 ):
-    wx, wy = sta.shape[0], sta.shape[1]
+    wx, wy = start_ref.shape[0], start_ref.shape[1]
     ex, ey = wx + 2 * H, wy + 2 * H
     o = 2 * H
     mid_x, mid_y = pl.ds(H, wx), pl.ds(o, wy)
@@ -78,17 +137,17 @@
         (yh_ref, fld.at[:, mid_x, high_y]),
         (xl_ref, fld.at[:, low_x, mid_y]),
         (xh_ref, fld.at[:, high_x, mid_y]),
-        (cl_ref.at[:, :, pl.ds(0, H)], fld.at[:, low_x, low_y]),
-        (cl_ref.at[:, :, pl.ds(H, H)], fld.at[:, low_x, high_y]),
-        (ch_ref.at[:, :, pl.ds(0, H)], fld.at[:, high_x, low_y]),
-        (ch_ref.at[:, :, pl.ds(H, H)], fld.at[:, high_x, high_y]),
-        (start_ref, sta),
-        (prior_ref, pri),
     ]
     copies = [pltpu.make_async_copy(src, dst, sems.at[k]) for k, (src, dst) in enumerate(copies)]
     for c in copies:
         c.start()
-    for c in copies[:10]:
+    for at, d, f, n in corner_rows():
+        fld[f, H - d, o - n : o, :] = cl_ref[at : at + n, :]
+        fld[f, H - d, o + wy : o + wy + n, :] = ch_ref[at : at + n, :]
+        at += CORNER // 2
+        fld[f, H + wx - 1 + d, o - n : o, :] = cl_ref[at : at + n, :]
+        fld[f, H + wx - 1 + d, o + wy : o + wy + n, :] = ch_ref[at : at + n, :]
+    for c in copies:
         c.wait()
 
     x_low, x_high, y_low, y_high = (sides_ref[k] for k in range(4))
@@ -132,25 +191,23 @@
 
     for step in range(STEPS):
         side = STEPS - 1 - step
-        for k in range(side):
-            rows_of(step, H - 1 - k, 1, x_low)
-            rows_of(step, H + wx + k, 1, x_high)
+        if side:
+            rows_of(step, H - side, side, x_low)
+            rows_of(step, H + wx, side, x_high)
 
         def some(i, carry, step=step):
-            rows_of(step, H + i * 2, 2, None)
+            rows_of(step, H + i * 8, 8, None)
             return carry
 
-        lax.fori_loop(0, wx // 2, some, 0)
-
-    for c in copies[10:]:
-        c.wait()
+        lax.fori_loop(0, wx // 8, some, 0)
+
     blocks = wy // 8
     groups = wx * blocks
 
     def load(f, g):
         if f < 8:
-            return tile_of(pri, f, g, blocks)
-        return tile_of(sta, None, g, blocks) if f == 8 else tile_of(basis_ref, f - 9, g, blocks)
+            return tile_of(prior_ref, f, g, blocks)
+        return tile_of(start_ref, None, g, blocks) if f == 8 else tile_of(basis_ref, f - 9, g, blocks)
 
     n = len(EARLY)
     acc[0 : n * 8, :] = early_ref[...].reshape(n * 8, 128)
@@ -175,24 +232,12 @@
 
 def combine_kernel(
     count, chunks,
-    sums_ref, first_ref, second_ref, start_hbm, basis_hbm, prior_hbm,
+    sums_ref, first_ref, second_ref, start_ref, basis_ref, prior_ref,
     new_hbm, coeffs_ref,
-    bas, pri, new, spread, in_sems, out_sems,
+    new, spread, out_sems,
 ):
-    wx, wy = bas.shape[1], bas.shape[2]
+    wx, wy = start_ref.shape[0], start_ref.shape[1]
     part = wx // chunks
-    loads = []
-    for k in range(chunks):
-        xs = pl.ds(k * part, part)
-        loads.append([
-            pltpu.make_async_copy(start_hbm.at[xs], bas.at[0, xs], in_sems.at[k, 0]),
-            pltpu.make_async_copy(basis_hbm.at[:, xs], bas.at[pl.ds(1, STEPS), xs], in_sems.at[k, 1]),
-            pltpu.make_async_copy(prior_hbm.at[:, xs], pri.at[:, xs], in_sems.at[k, 2]),
-        ])
-    for group in loads:
-        for c in group:
-            c.start()
-
     total = sums_ref[0:8, :]
     for k in range(1, sums_ref.shape[0] // 8):
         total = total + sums_ref[k * 8 : k * 8 + 8, :]
@@ -222,21 +267,21 @@
         scaled = work[k : k + 1, :] / jnp.sqrt(pivot)
         column = work[:, k : k + 1] / pivot
         work = jnp.where(row > k, work - column * work[k : k + 1, :], jnp.where(row == k, scaled, work))
-    coeffs_ref[0:PRIOR, :] = pltpu.roll(top, 128 - PRIOR, 1)[:, :NEW]
-    coeffs_ref[PRIOR:FIELDS, :] = jnp.where(lane >= row, work, 0.0)[:NEW, :NEW]
+    upper = jnp.where((lane >= row) & (lane < NEW), work, 0.0)
+    both = jnp.concatenate([pltpu.roll(top, 128 - PRIOR, 1), upper], axis=0)
+    both = jnp.concatenate([both, jnp.zeros((104, 128), jnp.float32)], axis=0)
+    coeffs_ref[...] = both.T[:NEW, :FIELDS]
     for i in range(FIELDS):
         at = 16 + i if i < NEW else 32 + i - NEW
         spread[i] = jnp.broadcast_to(work[:, at : at + 1], (16, 128))
 
     stores = []
     for k in range(chunks):
-        for c in loads[k]:
-            c.wait()
-
         def some(g, carry, k=k):
             x, y = k * part + g // (wy // 16), g % (wy // 16)
             ys = pl.ds(pl.multiple_of(y * 16, 16), 16)
-            tiles = [bas[i, x, ys, :] for i in range(NEW)] + [pri[i, x, ys, :] for i in range(PRIOR)]
+            tiles = [start_ref[x, ys, :]] + [basis_ref[i, x, ys, :] for i in range(STEPS)]
+            tiles += [prior_ref[i, x, ys, :] for i in range(PRIOR)]
             for j in range(NEW):
                 r = spread[0, j : j + 1, :] * tiles[0]
                 for i in range(1, j + 1):
@@ -261,54 +306,75 @@
     ahead_x, ahead_y = ([(i, i + 1) for i in range(n - 1)] for n in (nx, ny))
     back_x, back_y = ([(i + 1, i) for i in range(n - 1)] for n in (nx, ny))
 
-    def edge(at, dim):
-        cut = [slice(None)] * 3
-        cut[dim] = slice(at, at + H)
-        return jnp.concatenate([start[tuple(cut)][None], velocity[(slice(None), *cut)]], axis=0)
-
-    yl = lax.ppermute(edge(wy - H, 1), "gy", ahead_y)
-    yh = lax.ppermute(edge(0, 1), "gy", back_y)
-    xl = lax.ppermute(edge(wx - H, 0), "gx", ahead_x)
-    xh = lax.ppermute(edge(0, 0), "gx", back_x)
-    cl = lax.ppermute(jnp.concatenate([yl[:, wx - H :], yh[:, wx - H :]], axis=2), "gx", ahead_x)
-    ch = lax.ppermute(jnp.concatenate([yl[:, :H], yh[:, :H]], axis=2), "gx", back_x)
-    ix, iy = lax.axis_index("gx"), lax.axis_index("gy")
-    sides = jnp.stack([ix > 0, ix < nx - 1, iy > 0, iy < ny - 1]).astype(jnp.float32)
-
     f32 = jnp.float32
     vmem = pl.BlockSpec(memory_space=pltpu.VMEM)
     smem = pl.BlockSpec(memory_space=pltpu.SMEM)
     hbm = pl.BlockSpec(memory_space=pl.ANY)
-    limit = pltpu.CompilerParams(vmem_limit_bytes=48 * 1024 * 1024)
-    early = pl.pallas_call(
+    limit = pltpu.CompilerParams(vmem_limit_bytes=32 * 1024 * 1024)
+    edge_y = jax.ShapeDtypeStruct((4, wx, H, wz), f32)
+    edge_x = jax.ShapeDtypeStruct((4, H, wy, wz), f32)
+    corner = jax.ShapeDtypeStruct((CORNER, wz), f32)
+    start_hbm, velocity_hbm, prior_hbm = (
+        pltpu.with_memory_space_constraint(v, pltpu.HBM) for v in (start, velocity, prior)
+    )
+    y_first, y_last, x_first, x_last = pl.pallas_call(
+        pack_kernel,
+        out_shape=(edge_y, edge_y, edge_x, edge_x),
+        in_specs=[hbm, hbm],
+        out_specs=(vmem,) * 4,
+        scratch_shapes=[pltpu.SemaphoreType.DMA((8,))],
+        compiler_params=limit,
+        name="pack",
+    )(start_hbm, velocity_hbm)
+    xl = lax.ppermute(x_last, "gx", ahead_x)
+    xh = lax.ppermute(x_first, "gx", back_x)
+    yl = lax.ppermute(y_last, "gy", ahead_y)
+    yh = lax.ppermute(y_first, "gy", back_y)
+    to_up, to_down = pl.pallas_call(
+        corner_kernel,
+        out_shape=(corner, corner),
+        in_specs=[vmem, vmem],
+        out_specs=(vmem, vmem),
+        compiler_params=limit,
+        name="corner",
+    )(xl, xh)
+    cl = lax.ppermute(to_up, "gy", ahead_y)
+    ch = lax.ppermute(to_down, "gy", back_y)
+    early, prior_in, start_in = pl.pallas_call(
         early_kernel,
-        out_shape=jax.ShapeDtypeStruct((len(EARLY), 8, 128), f32),
-        in_specs=[vmem, vmem],
-        out_specs=vmem,
+        out_shape=(
+            jax.ShapeDtypeStruct((len(EARLY), 8, 128), f32),
+            pltpu.VMEM(prior.shape, f32),
+            pltpu.VMEM(start.shape, f32),
+        ),
+        in_specs=[hbm, hbm],
+        out_specs=(vmem, vmem, vmem),
+        scratch_shapes=[pltpu.SemaphoreType.DMA((4, 2))],
         compiler_params=limit,
         name="early",
-    )(prior, start)
+    )(prior_hbm, start_hbm)
+    ix, iy = lax.axis_index("gx"), lax.axis_index("gy")
+    sides = jnp.stack([ix > 0, ix < nx - 1, iy > 0, iy < ny - 1]).astype(jnp.float32)
+
     ex, ey = wx + 2 * H, wy + 4 * H
     basis, sums = pl.pallas_call(
         stencil_kernel,
         out_shape=(
-            jax.ShapeDtypeStruct((STEPS, wx, wy, wz), f32),
+            pltpu.VMEM((STEPS, wx, wy, wz), f32),
             jax.ShapeDtypeStruct((devices * 2, 128), f32),
         ),
-        in_specs=[smem, smem] + [hbm] * 9 + [vmem],
+        in_specs=[smem, smem, vmem] + [hbm] * 5 + [vmem] * 4,
         out_specs=(vmem, vmem),
         scratch_shapes=[
             pltpu.VMEM((4, ex, ey, wz), f32),
             pltpu.VMEM((ex, ey, wz), f32),
             pltpu.VMEM((ex, ey, wz), f32),
-            pltpu.VMEM((PRIOR, wx, wy, wz), f32),
-            pltpu.VMEM((wx, wy, wz), f32),
             pltpu.VMEM((SLOTS * 8, 128), f32),
-            pltpu.SemaphoreType.DMA((12,)),
+            pltpu.SemaphoreType.DMA((6,)),
         ],
         compiler_params=limit,
         name="stencil",
-    )(shifts, sides, start, velocity, yl, yh, xl, xh, cl, ch, prior, early)
+    )(shifts, sides, start_in, velocity_hbm, yl, yh, xl, xh, cl, ch, prior_in, early)
     every = lax.all_to_all(sums, AXES, 0, 0, tiled=True)
     chunks = 4
     first, second = pair_tables()
@@ -316,22 +382,19 @@
         functools.partial(combine_kernel, float(devices * wx * wy * wz), chunks),
         out_shape=(
             jax.ShapeDtypeStruct((NEW, wx, wy, wz), f32),
-            jax.ShapeDtypeStruct((FIELDS, NEW), f32),
+            jax.ShapeDtypeStruct((NEW, FIELDS), f32),
         ),
-        in_specs=[vmem, vmem, vmem, hbm, hbm, hbm],
+        in_specs=[vmem] * 6,
         out_specs=(hbm, vmem),
         scratch_shapes=[
             pltpu.VMEM((NEW, wx, wy, wz), f32),
-            pltpu.VMEM((PRIOR, wx, wy, wz), f32),
-            pltpu.VMEM((NEW, wx, wy, wz), f32),
             pltpu.VMEM((FIELDS, 16, 128), f32),
-            pltpu.SemaphoreType.DMA((chunks, 3)),
             pltpu.SemaphoreType.DMA((chunks,)),
         ],
         compiler_params=limit,
         name="combine",
-    )(every, jnp.asarray(first), jnp.asarray(second), start, basis, prior)
-    return basis_new, coeffs
+    )(every, jnp.asarray(first), jnp.asarray(second), start_in, basis, prior_in)
+    return basis_new, coeffs.T
 
 
 def solution(mesh):

time: 103 us -> 83.4 us (0.81)
  Pallas kernels: 35.8 us -> 27.5 us
  local copies, waits for them, and re-layouts: 7.52 us -> 0.01 us
  other arithmetic: 3.29 us -> 0.08 us
  starting transfers between devices: 18.1 us -> 15.4 us
  blocking collectives: 30.5 us -> 32.2 us
    pallas_call x2 -> x4, Pallas kernels: 27.3 us -> 19.4 us  [the longest x1 13.9 us: on_device(): pl.pallas_call(stencil_kernel, out_shape=(pltpu.VMEM((STEPS, wx, wy, wz),...]
    unnamed x14 -> x6, local copies, waits for them, and re-layouts: 4.39 us -> 0.01 us
    concatenate x6 -> x0, other arithmetic: 3.2 us -> none  [the longest x4 1.76 us: edge(): jnp.concatenate([start[tuple(cut)][None], velocity[slice(None), *cut]], a...]
    ppermute x6, starting transfers between devices: 18.1 us -> 15.4 us  [the longest x1 4.51 us: on_device(): xl = lax.ppermute(x_last, 'gx', ahead_x)]
    all_to_all x1, blocking collectives: 30.5 us -> 32.2 us  [on_device(): every = lax.all_to_all(sums, AXES, 0, 0, tiled=True)]
    slice x4 -> x0, local copies, waits for them, and re-layouts: 1.29 us -> none  [the longest x2 1.25 us: edge(): velocity[slice(None), *cut]]
    broadcast_in_dim x2 -> x0, local copies, waits for them, and re-layouts: 1.15 us -> none  [edge(): start[tuple(cut)][None]]
  transfers between devices with their start and end apart: 6 -> 6, of which waited for: 3 -> 3; matrix products, arithmetic and copies ran while one was open for 3% -> 0% of each run, Pallas kernels for 3% -> 5%
where the time goes in v1:
time: 83.4 us; the launch traced here: 83.1 us
  blocking collectives  32.2 us (39%)
  Pallas kernels  27.5 us (33%)
  starting transfers between devices  15.4 us (18%)
  waiting for transfers between devices  7.14 us (9%)
    all_to_all x1, blocking collectives, on_device(): every = lax.all_to_all(sums, AXES, 0, 0, tiled=True)  32.2 us
    pallas_call x1, Pallas kernels, on_device(): pl.pallas_call(stencil_kernel, out_shape=(pltpu.VMEM((STEPS, wx, wy, wz),...  13.9 us
    pallas_call x1, Pallas kernels, on_device(): pl.pallas_call(functools.partial(combine_kernel, float(devices * wx * wy...  8.14 us
    ppermute x1, starting transfers between devices, on_device(): xl = lax.ppermute(x_last, 'gx', ahead_x)  4.51 us
    ppermute x1, waiting for transfers between devices, on_device(): xh = lax.ppermute(x_first, 'gx', back_x)  4.31 us
    ppermute x1, starting transfers between devices, on_device(): cl = lax.ppermute(to_up, 'gy', ahead_y)  3.19 us
    ppermute x1, starting transfers between devices, on_device(): yl = lax.ppermute(y_last, 'gy', ahead_y)  3.19 us
    pallas_call x1, Pallas kernels, on_device(): pl.pallas_call(early_kernel, out_shape=(jax.ShapeDtypeStruct((len(EARLY),...  3.13 us
  transfers between devices with their start and end apart: 6, of which 3 were waited for; matrix products, arithmetic and copies ran while one was open for 0% of the time, Pallas kernels for 5%

profile of v1, /device:TPU:1, one launch (start us, length us, event | category | flops | bytes accessed | tf_op | source)
XLA Modules:
  0.0 83.1 jit_solution(9091745574739664374)
XLA Ops:
  0.6 0.0 copy-start.2
  0.6 1.6 %pack.1 = (f32[4,32,8,128]{3,2,1,0:T(8,128)S(1)}, f32[4,32,8,128]{3,2,1,0:T(8,128)S(1)}, f32[4,8,32,128]{3,2,1,0:T(8,128)S(1)}, f32[4,8,32,128]{3,2,1,0:T(8,128)S(1)}) custom-call(f32[32,32,128]{2,1,0:T(8,128)} %start_ref.1, f32[3,32,32,128]{3,2,1,0:T(8,128)} %vel_ref.3), custom_call_target="tpu_custom_call" | custom-call | tf_op jit(solution)/shard_map/pack/pallas_call | solution.py:320
  2.3 4.5 %collective-permute-start.2 = (f32[4,8,32,128]{3,2,1,0:T(8,128)S(1)}, f32[4,8,32,128]{3,2,1,0:T(8,128)S(1)}, u32[]{:S(2)}, u32[]{:S(2)}) collective-permute-start(f32[4,8,32,128]{3,2,1,0:T(8,128)S(1)} %get-tuple-element.18), channel_id=1, source_target_pairs={{0,32},{32,64},{64,96},{96,128},{128,160},{160,192},{192,224},{1,3... | collective-permute-start | bytes 1572872 | tf_op jit(solution)/shard_map/ppermute | solution.py:329
  6.8 2.0 %collective-permute-start.3 = (f32[4,8,32,128]{3,2,1,0:T(8,128)S(1)}, f32[4,8,32,128]{3,2,1,0:T(8,128)S(1)}, u32[]{:S(2)}, u32[]{:S(2)}) collective-permute-start(f32[4,8,32,128]{3,2,1,0:T(8,128)S(1)} %get-tuple-element.19), channel_id=1, source_target_pairs={{32,0},{64,32},{96,64},{128,96},{160,128},{192,160},{224,192},{33,... | collective-permute-start | bytes 1572872 | tf_op jit(solution)/shard_map/ppermute | solution.py:330
  8.8 3.2 %collective-permute-start = (f32[4,32,8,128]{3,2,1,0:T(8,128)S(1)}, f32[4,32,8,128]{3,2,1,0:T(8,128)S(1)}, u32[]{:S(2)}, u32[]{:S(2)}) collective-permute-start(f32[4,32,8,128]{3,2,1,0:T(8,128)S(1)} %get-tuple-element.16), channel_id=1, source_target_pairs={{0,1},{1,2},{2,3},{3,4},{4,5},{5,6},{6,7},{7,8},{8,9},{9,10},{10,1... | collective-permute-start | bytes 1572872 | tf_op jit(solution)/shard_map/ppermute | solution.py:331
  12.0 1.3 %collective-permute-start.1 = (f32[4,32,8,128]{3,2,1,0:T(8,128)S(1)}, f32[4,32,8,128]{3,2,1,0:T(8,128)S(1)}, u32[]{:S(2)}, u32[]{:S(2)}) collective-permute-start(f32[4,32,8,128]{3,2,1,0:T(8,128)S(1)} %get-tuple-element.17), channel_id=1, source_target_pairs={{1,0},{2,1},{3,2},{4,3},{5,4},{6,5},{7,6},{8,7},{9,8},{10,9},{11,1... | collective-permute-start | bytes 1572872 | tf_op jit(solution)/shard_map/ppermute | solution.py:332
  13.3 0.0 collective-permute-done.2.xl_ref
  13.3 4.3 %collective-permute-done.3.xh_ref = f32[4,8,32,128]{3,2,1,0:T(8,128)S(1)} collective-permute-done((f32[4,8,32,128]{3,2,1,0:T(8,128)S(1)}, f32[4,8,32,128]{3,2,1,0:T(8,128)S(1)}, u32[]{:S(2)}, u32[]{:S(2)}) %collective-permute-start.3) | collective-permute-done | bytes 524320 | tf_op jit(solution)/shard_map/ppermute | solution.py:330
  17.6 0.7 corner.1
  18.3 3.2 %collective-permute-start.4 = (f32[224,128]{1,0:T(8,128)}, f32[224,128]{1,0:T(8,128)S(1)}, u32[]{:S(2)}, u32[]{:S(2)}) collective-permute-start(f32[224,128]{1,0:T(8,128)} %get-tuple-element.20), channel_id=1, source_target_pairs={{0,1},{1,2},{2,3},{3,4},{4,5},{5,6},{6,7},{7,8},{8,9},{9,10},{10,1... | collective-permute-start | bytes 344072 | tf_op jit(solution)/shard_map/ppermute | solution.py:341
  21.5 1.3 %collective-permute-start.5 = (f32[224,128]{1,0:T(8,128)S(1)}, f32[224,128]{1,0:T(8,128)S(1)}, u32[]{:S(2)}, u32[]{:S(2)}) collective-permute-start(f32[224,128]{1,0:T(8,128)S(1)} %get-tuple-element.21), channel_id=1, source_target_pairs={{1,0},{2,1},{3,2},{4,3},{5,4},{6,5},{7,6},{8,7},{9,8},{10,9},{11,1... | collective-permute-start | bytes 344072 | tf_op jit(solution)/shard_map/ppermute | solution.py:342
  22.8 3.1 %early.1 = (f32[45,8,128]{2,1,0:T(8,128)S(1)}, f32[8,32,32,128]{3,2,1,0:T(8,128)S(1)}, f32[32,32,128]{2,1,0:T(8,128)S(1)}) custom-call(f32[8,32,32,128]{3,2,1,0:T(8,128)} %prior_hbm.1, f32[32,32,128]{2,1,0:T(8,128)} %start_ref.1), custom_call_target="tpu_custom_call" | custom-call | tf_op jit(solution)/shard_map/early/pallas_call | solution.py:343
  25.9 0.1 add_convert_fusion.sides_ref
  26.0 0.0 collective-permute-done.yl_ref
  26.0 1.8 %collective-permute-done.1.yh_ref = f32[4,32,8,128]{3,2,1,0:T(8,128)S(1)} collective-permute-done((f32[4,32,8,128]{3,2,1,0:T(8,128)S(1)}, f32[4,32,8,128]{3,2,1,0:T(8,128)S(1)}, u32[]{:S(2)}, u32[]{:S(2)}) %collective-permute-start.1) | collective-permute-done | bytes 524320 | tf_op jit(solution)/shard_map/ppermute | solution.py:332
  27.8 0.0 collective-permute-done.4.cl_ref
  27.8 1.0 %collective-permute-done.5.ch_ref = f32[224,128]{1,0:T(8,128)S(1)} collective-permute-done((f32[224,128]{1,0:T(8,128)S(1)}, f32[224,128]{1,0:T(8,128)S(1)}, u32[]{:S(2)}, u32[]{:S(2)}) %collective-permute-start.5) | collective-permute-done | bytes 114720 | tf_op jit(solution)/shard_map/ppermute | solution.py:342
  28.8 0.0 copy-done.2
  28.8 0.0 copy-start
  28.9 0.0 copy-start.1
  28.9 13.9 %stencil.1 = (f32[8,32,32,128]{3,2,1,0:T(8,128)S(1)}, f32[512,128]{1,0:T(8,128)S(1)}) custom-call(f32[8]{0:T(128)S(1)} %copy-done.2, f32[4]{0:T(128)S(1)} %add_convert_fusion.sides_ref, f32[32,32,128]{2,1,0:T(8,128)S(1)} %get-tuple-element.15.start_ref, f32[3,32,32,128]{3,2,1,0:T(8,128)} %vel_ref.3, f32[4,32,8,128]{3,2,1,0:T(8,128)S(1)} %collective-permute-done.yl_ref, ...), custom_call_target="tpu_custom_call" | custom-call | tf_op jit(solution)/shard_map/stencil/pallas_call | solution.py:360
  42.8 32.2 %all_to_all.11 = f32[256,2,128]{2,1,0:T(2,128)S(1)} all-to-all(f32[256,2,128]{2,1,0:T(2,128)S(1)} %bitcast.8), channel_id=1, replica_groups=mesh['gx'=8,'gy'=32] {'gx','gy'}, dimensions={0} | all-to-all | bytes 524288 | tf_op jit(solution)/shard_map/all_to_all | solution.py:378
  74.9 0.0 copy-done
  74.9 0.0 copy-done.1
  74.9 8.1 %combine.1 = (f32[9,32,32,128]{3,2,1,0:T(8,128)}, f32[9,17]{1,0:T(8,128)}) custom-call(f32[512,128]{1,0:T(8,128)S(1)} %bitcast.7, f32[128,256]{1,0:T(8,128)S(1)} %copy-done.1, f32[128,256]{1,0:T(8,128)S(1)} %copy-done, f32[32,32,128]{2,1,0:T(8,128)S(1)} %get-tuple-element.15.start_ref, f32[8,32,32,128]{3,2,1,0:T(8,128)S(1)} %get-tuple-element.25.basis_ref, ...), custom_call_target="tpu_custom_call" | custom-call | tf_op jit(solution)/shard_map/combine/pallas_call | solution.py:381
Async XLA Ops:
  0.6 28.2 %copy-start.2 = (f32[8]{0:T(128)S(1)}, f32[8]{0:T(128)}, u32[]{:S(2)}) copy-start(f32[8]{0:T(128)} %shifts_ref.1) | copy-start | bytes 100
  2.3 11.0 %collective-permute-start.2 = (f32[4,8,32,128]{3,2,1,0:T(8,128)S(1)}, f32[4,8,32,128]{3,2,1,0:T(8,128)S(1)}, u32[]{:S(2)}, u32[]{:S(2)}) collective-permute-start(f32[4,8,32,128]{3,2,1,0:T(8,128)S(1)} %get-tuple-element.18), channel_id=1, source_target_pairs={{0,32},{32,64},{64,96},{96,128},{128,160},{160,192},{192,224},{1,3... | collective-permute-start | bytes 1572872 | tf_op jit(solution)/shard_map/ppermute | solution.py:329
  6.8 10.8 %collective-permute-start.3 = (f32[4,8,32,128]{3,2,1,0:T(8,128)S(1)}, f32[4,8,32,128]{3,2,1,0:T(8,128)S(1)}, u32[]{:S(2)}, u32[]{:S(2)}) collective-permute-start(f32[4,8,32,128]{3,2,1,0:T(8,128)S(1)} %get-tuple-element.19), channel_id=1, source_target_pairs={{32,0},{64,32},{96,64},{128,96},{160,128},{192,160},{224,192},{33,... | collective-permute-start | bytes 1572872 | tf_op jit(solution)/shard_map/ppermute | solution.py:330
  8.8 17.3 %collective-permute-start = (f32[4,32,8,128]{3,2,1,0:T(8,128)S(1)}, f32[4,32,8,128]{3,2,1,0:T(8,128)S(1)}, u32[]{:S(2)}, u32[]{:S(2)}) collective-permute-start(f32[4,32,8,128]{3,2,1,0:T(8,128)S(1)} %get-tuple-element.16), channel_id=1, source_target_pairs={{0,1},{1,2},{2,3},{3,4},{4,5},{5,6},{6,7},{7,8},{8,9},{9,10},{10,1... | collective-permute-start | bytes 1572872 | tf_op jit(solution)/shard_map/ppermute | solution.py:331
  12.0 15.9 %collective-permute-start.1 = (f32[4,32,8,128]{3,2,1,0:T(8,128)S(1)}, f32[4,32,8,128]{3,2,1,0:T(8,128)S(1)}, u32[]{:S(2)}, u32[]{:S(2)}) collective-permute-start(f32[4,32,8,128]{3,2,1,0:T(8,128)S(1)} %get-tuple-element.17), channel_id=1, source_target_pairs={{1,0},{2,1},{3,2},{4,3},{5,4},{6,5},{7,6},{8,7},{9,8},{10,9},{11,1... | collective-permute-start | bytes 1572872 | tf_op jit(solution)/shard_map/ppermute | solution.py:332
  18.3 9.5 %collective-permute-start.4 = (f32[224,128]{1,0:T(8,128)}, f32[224,128]{1,0:T(8,128)S(1)}, u32[]{:S(2)}, u32[]{:S(2)}) collective-permute-start(f32[224,128]{1,0:T(8,128)} %get-tuple-element.20), channel_id=1, source_target_pairs={{0,1},{1,2},{2,3},{3,4},{4,5},{5,6},{6,7},{7,8},{8,9},{9,10},{10,1... | collective-permute-start | bytes 344072 | tf_op jit(solution)/shard_map/ppermute | solution.py:341
  21.5 7.4 %collective-permute-start.5 = (f32[224,128]{1,0:T(8,128)S(1)}, f32[224,128]{1,0:T(8,128)S(1)}, u32[]{:S(2)}, u32[]{:S(2)}) collective-permute-start(f32[224,128]{1,0:T(8,128)S(1)} %get-tuple-element.21), channel_id=1, source_target_pairs={{1,0},{2,1},{3,2},{4,3},{5,4},{6,5},{7,6},{8,7},{9,8},{10,9},{11,1... | collective-permute-start | bytes 344072 | tf_op jit(solution)/shard_map/ppermute | solution.py:342
  28.8 46.1 %copy-start = (f32[128,256]{1,0:T(8,128)S(1)}, f32[128,256]{1,0:T(8,128)}, u32[]{:S(2)}) copy-start(f32[128,256]{1,0:T(8,128)} %constant.20.clone.second_ref) | copy-start | bytes 393220
  28.9 46.1 %copy-start.1 = (f32[128,256]{1,0:T(8,128)S(1)}, f32[128,256]{1,0:T(8,128)}, u32[]{:S(2)}) copy-start(f32[128,256]{1,0:T(8,128)} %constant.19.clone.first_ref) | copy-start | bytes 393220

commit v2 on v1

v2 whole, which is shorter than its diff:
```python
import functools

import jax
import jax.numpy as jnp
import numpy as np
from jax import lax
from jax.experimental import pallas as pl
from jax.experimental.pallas import tpu as pltpu
from jax.sharding import PartitionSpec as P

STEPS = 8
PRIOR = 8
NEW = STEPS + 1
FIELDS = PRIOR + NEW
H = STEPS
DRIFT = 0.3
SIXTH = 1.0 / 6.0
AXES = ("gx", "gy")

EARLY = [(i, j) for i in range(9) for j in range(i, 9)]
LATE = [(i, j) for i in range(9, 17) for j in range(i, 17)]
CROSS = [[(i, j) for i in range(9) for j in range(lo, lo + 4)] for lo in (9, 13)]
PAIRS = EARLY + LATE + CROSS[0] + CROSS[1]
SLOTS = 160


def pair_tables():
    first = np.zeros((128, 256), np.float32)
    second = np.zeros((128, 256), np.float32)
    for p, (i, j) in enumerate(PAIRS):
        first[i, p] = 0.5 if i == j else 1.0
        second[j, p] = 1.0
    return first, second


def corner_rows():
    at, pieces = 0, []
    for d in range(1, H):
        for f in range(4):
            n = H - d if f == 0 else H - 1 - d
            if n:
                pieces.append((at, d, f, n))
            at += n
    return pieces


CORNER = 2 * sum(n for _, _, _, n in corner_rows())


def pack_kernel(place_ref, start_ref, vel_ref, y_even, y_odd, x_even, x_odd, sems):
    wx, wy = start_ref.shape[0], start_ref.shape[1]
    full = slice(None)
    odd_x, odd_y = place_ref[4], place_ref[5]

    def cut(n, odd):
        return pl.ds(pl.multiple_of((n - H) * odd, H), H)

    copies = []
    for out, where in (
        (x_odd, (cut(wx, odd_x), full)),
        (x_even, (cut(wx, 1 - odd_x), full)),
        (y_odd, (full, cut(wy, odd_y))),
        (y_even, (full, cut(wy, 1 - odd_y))),
    ):
        copies.append((start_ref.at[where], out.at[0]))
        copies.append((vel_ref.at[(full, *where)], out.at[pl.ds(1, 3)]))
    copies = [pltpu.make_async_copy(src, dst, sems.at[k]) for k, (src, dst) in enumerate(copies)]
    for c in copies:
        c.start()
    for c in copies:
        c.wait()


def corner_kernel(place_ref, xe_ref, xo_ref, even_ref, odd_ref):
    wy = xe_ref.shape[2]
    odd_x, odd_y = place_ref[4] == 1, place_ref[5] == 1

    def put(at, f, row, n, low):
        for_low, for_high = (xe_ref, xo_ref) if low else (xo_ref, xe_ref)
        last = jnp.where(odd_x, for_low[f, row, wy - n :, :], for_high[f, row, wy - n :, :])
        first = jnp.where(odd_x, for_low[f, row, :n, :], for_high[f, row, :n, :])
        even_ref[at : at + n, :] = jnp.where(odd_y, first, last)
        odd_ref[at : at + n, :] = jnp.where(odd_y, last, first)

    for at, d, f, n in corner_rows():
        put(at, f, H - d, n, True)
        put(at + CORNER // 2, f, d - 1, n, False)


def products(load, pairs, groups, start=None):
    used = sorted({f for pair in pairs for f in pair})

    def body(g, totals):
        tile = {f: load(f, g) for f in used}
        return tuple(t + tile[i] * tile[j] for t, (i, j) in zip(totals, pairs))

    if start is None:
        start = (jnp.zeros((8, 128), jnp.float32),) * len(pairs)
    return lax.fori_loop(0, groups, body, start, unroll=8)


def early_kernel(prior_hbm, start_hbm, vel_hbm, out_ref, prior_ref, field, flow, sems):
    wx, wy = prior_ref.shape[1], prior_ref.shape[2]
    blocks = wy // 8
    parts = sems.shape[0] - 1
    part = wx // parts
    copies = []
    for k in range(parts):
        xs = pl.ds(k * part, part)
        inside = field.at[pl.ds(H + k * part, part), pl.ds(H, wy)]
        copies.append([
            pltpu.make_async_copy(prior_hbm.at[:, xs], prior_ref.at[:, xs], sems.at[k, 0]),
            pltpu.make_async_copy(start_hbm.at[xs], inside, sems.at[k, 1]),
        ])
        for c in copies[-1]:
            c.start()
    last = pltpu.make_async_copy(vel_hbm, flow.at[:, pl.ds(H, wx)], sems.at[parts, 0])
    last.start()

    totals = None
    for k in range(parts):
        for c in copies[k]:
            c.wait()

        def load(f, g, k=k):
            x, y = k * part + g // blocks, g % blocks * 8
            if f < 8:
                return prior_ref[f, x, pl.ds(pl.multiple_of(y, 8), 8), :]
            return field[H + x, pl.ds(pl.multiple_of(H + y, 8), 8), :]

        totals = products(load, EARLY, part * blocks, totals)
    for p, total in enumerate(totals):
        out_ref[p] = total
    last.wait()


def side(low, near, far):
    return pl.ds(pl.multiple_of(far - low * (far - near), H), H)


def coefficients(flow):
    lane = lax.broadcasted_iota(jnp.int32, (1, 1, 128), 2)
    a2 = DRIFT * flow[2]
    up = jnp.where(lane < 127, a2 - SIXTH, 0.0)
    down = jnp.where(lane > 0, -a2 - SIXTH, 0.0)
    return DRIFT * flow[0], DRIFT * flow[1], up, down


def stepped(src, x, n, y, size, keep, coefficient):
    here, ys = pl.ds(x, n), pl.ds(y, size)
    c = src[here, ys, :]
    e, w = src[pl.ds(x + 1, n), ys, :], src[pl.ds(x - 1, n), ys, :]
    u, d = src[here, pl.ds(y + 1, size), :], src[here, pl.ds(y - 1, size), :]
    a0, a1, up, down = coefficient
    above, below = pltpu.roll(c, 127, 2), pltpu.roll(c, 1, 2)
    return keep * c - SIXTH * ((e + w) + (u + d)) + a0 * (e - w) + a1 * (u - d) + (up * above + down * below)


def over_x(step, wx, rows, scale_low, scale_high, ready=None):
    def some(n):
        def body(i, carry):
            for k in range(0, n, 2):
                rows(H + (2 if ready else 0) + i * n + k, 2, None)
            return carry

        return body

    if ready:
        lax.fori_loop(0, 2, some(wx // 2 - 2), 0)
        ready()
        rows(H, 2, None)
        rows(H + wx - 2, 2, None)
    halo = STEPS - 1 - step
    for k in range(0, halo, 2):
        n = min(2, halo - k)
        rows(H - halo + k, n, scale_low)
        rows(H + wx + k, n, scale_high)
    if not ready:
        lax.fori_loop(0, wx // 16, some(16), 0)


def late_products(fields, prior_ref, wx, blocks, acc, start):
    count = len(blocks)
    gap = blocks[1] - blocks[0]

    def load(f, g):
        x, y = g // count, blocks[0] * 8 + g % count * (gap * 8)
        if f < 8:
            return prior_ref[f, x, pl.ds(pl.multiple_of(y, 8), 8), :]
        return fields[f - 8][H + x, pl.ds(pl.multiple_of(H + y, 8), 8), :]

    n = len(EARLY)
    for pairs in (LATE, *CROSS):
        before = None
        if not start:
            before = tuple(acc[(n + p) * 8 : (n + p) * 8 + 8, :] for p in range(len(pairs)))
        for p, total in enumerate(products(load, pairs, wx * count, before)):
            acc[(n + p) * 8 : (n + p) * 8 + 8, :] = total
        n += len(pairs)


def inner_kernel(
    shifts_ref, place_ref, xe_ref, xo_ref, prior_ref, early_ref, field_in, flow_in, *rest
):
    fields, (flow, low, high, acc, coef, sems) = rest[:NEW], rest[NEW:]
    wx, wy = prior_ref.shape[1], prior_ref.shape[2]
    mid_y = pl.ds(H, wy)
    odd_x = place_ref[4]
    even_at, odd_at = side(odd_x, 0, H + wx), side(1 - odd_x, 0, H + wx)
    copies = [
        (xe_ref.at[0], fields[0].at[even_at, mid_y]),
        (xo_ref.at[0], fields[0].at[odd_at, mid_y]),
        (xe_ref.at[pl.ds(1, 3)], flow.at[:, even_at]),
        (xo_ref.at[pl.ds(1, 3)], flow.at[:, odd_at]),
    ]
    copies = [pltpu.make_async_copy(src, dst, sems.at[k]) for k, (src, dst) in enumerate(copies)]
    for c in copies:
        c.start()
    n = len(EARLY)
    acc[0 : n * 8, :] = early_ref[...].reshape(n * 8, 128)

    def ready():
        for c in copies:
            c.wait()

    x_low, x_high = (place_ref[k].astype(jnp.float32) for k in range(2))
    for step in range(STEPS):
        keep = 1.0 - shifts_ref[step]
        skip = 0 if step < 3 else 4 if step < 7 else 8

        def rows(x, n, scale, step=step, keep=keep, skip=skip):
            here, size = pl.ds(x, n), wy - 2 * skip
            if step == 0:
                cs = coefficients([flow[k, here, :, :] for k in range(3)])
                for k in range(4):
                    coef[k, here, :, :] = cs[k]
                    low[k, here, H:, :] = cs[k][:, :H]
                    high[k, here, :H, :] = cs[k][:, wy - H :]
            else:
                cs = [coef[k, here, pl.ds(skip, size), :] for k in range(4)]
            r = stepped(fields[step], x, n, H + skip, size, keep, cs)
            fields[step + 1][here, pl.ds(H + skip, size), :] = r if scale is None else r * scale

        over_x(step, wx, rows, x_low, x_high, ready if step == 0 else None)
    late_products(fields, prior_ref, wx, range(1, wy // 8 - 1), acc, True)


def outer_kernel(
    shifts_ref, place_ref, yo_ref, ye_ref, co_ref, ce_ref, prior_ref, acc_ref, *rest
):
    low, high, *fields = rest[NEW + 2 : 2 * NEW + 4]
    sums_ref, flow, acc, sems = rest[2 * NEW + 4 :]
    wx, wy = prior_ref.shape[1], prior_ref.shape[2]
    mid_x = pl.ds(H, wx)
    odd_y = place_ref[5]
    copies = []
    for ref, first in ((ye_ref, odd_y), (yo_ref, 1 - odd_y)):
        copies.append((ref.at[0], fields[0].at[mid_x, side(first, 0, H + wy)]))
        copies.append((ref.at[pl.ds(1, 3)], flow.at[:, mid_x, side(first, 0, H)]))
    copies = [pltpu.make_async_copy(src, dst, sems.at[k]) for k, (src, dst) in enumerate(copies)]
    for c in copies:
        c.start()
    acc[...] = acc_ref[...]
    for at, d, f, n in corner_rows():
        for x in (H - d, H + wx - 1 + d):
            even, odd = ce_ref[at : at + n, :], co_ref[at : at + n, :]
            ahead, behind = jnp.where(odd_y == 1, even, odd), jnp.where(odd_y == 1, odd, even)
            if f == 0:
                fields[0][x, H - n : H, :] = ahead
                fields[0][x, H + wy : H + wy + n, :] = behind
            else:
                flow[f - 1, x, H - n : H, :] = ahead
                flow[f - 1, x, H : H + n, :] = behind
            at += CORNER // 2
    for c in copies:
        c.wait()

    def prepare(i, carry):
        for m in range(0, 16, 2):
            here = pl.ds(i * 16 + m, 2)
            for out, ys in ((low, pl.ds(0, H)), (high, pl.ds(H, H))):
                for k, c in enumerate(coefficients([flow[k, here, ys, :] for k in range(3)])):
                    out[k, here, ys, :] = c
        return carry

    lax.fori_loop(0, (wx + 2 * H) // 16, prepare, 0)
    x_low, x_high, y_low, y_high = (place_ref[k].astype(jnp.float32) for k in range(4))
    row = lax.broadcasted_iota(jnp.int32, (1, 8, 128), 1)
    for step in range(STEPS):
        keep = 1.0 - shifts_ref[step]
        windows = (
            (H + step - 7, low, step + 1, jnp.where(row < 7 - step, y_low, 1.0)),
            (H + wy - 1 - step, high, 7 - step, jnp.where(row > step, y_high, 1.0)),
        )

        def rows(x, n, scale, step=step, keep=keep, windows=windows):
            here = pl.ds(x, n)
            for at, coef, first, inside in windows:
                cs = [coef[k, here, pl.ds(first, 8), :] for k in range(4)]
                r = stepped(fields[step], x, n, at, 8, keep, cs)
                if step < STEPS - 1:
                    r = r * (inside if scale is None else inside * scale)
                fields[step + 1][here, pl.ds(at, 8), :] = r

        over_x(step, wx, rows, x_low, x_high)
    late_products(fields, prior_ref, wx, (0, wy // 8 - 1), acc, False)
    n = len(PAIRS)
    acc[n * 8 :, :] = jnp.zeros((SLOTS * 8 - n * 8, 128), jnp.float32)
    by_lane = acc[pl.ds(0, SLOTS, stride=8), :]
    for s in range(1, 8):
        by_lane = by_lane + acc[pl.ds(s, SLOTS, stride=8), :]
    total = lax.dot_general(
        jnp.ones((8, 128), jnp.float32), by_lane, (((1,), (1,)), ((), ())),
        precision=lax.Precision.HIGHEST, preferred_element_type=jnp.float32,
    )
    second = jnp.concatenate([total[:, 128:], jnp.zeros((8, 256 - SLOTS), jnp.float32)], axis=1)
    even = lax.broadcasted_iota(jnp.int32, (8, 128), 0) % 2 == 0
    both = jnp.where(even, total[:, :128], second)
    sums_ref[...] = both


def combine_kernel(
    count, chunks, sums_ref, first_ref, second_ref, prior_ref, *rest
):
    fields, (new_hbm, coeffs_ref, new, spread, out_sems) = rest[:NEW], rest[NEW:]
    wx, wy = prior_ref.shape[1], prior_ref.shape[2]
    part = wx // chunks
    total = sums_ref[0:8, :]
    for k in range(1, sums_ref.shape[0] // 8):
        total = total + sums_ref[k * 8 : k * 8 + 8, :]
    total = total + pltpu.roll(total, 4, 0)
    total = (total + pltpu.roll(total, 2, 0)) * (1.0 / count)
    flat = jnp.concatenate([total[0:1, :], total[1:2, :]], axis=1)
    contract = functools.partial(
        lax.dot_general, dimension_numbers=(((1,), (1,)), ((), ())),
        precision=lax.Precision.HIGHEST, preferred_element_type=jnp.float32,
    )
    first, second = first_ref[...], second_ref[...]
    full = contract(first[:24] * flat, second) + contract(second[:24] * flat, first)
    top, low = full[0:8, :], full[8:24, :]
    inner = 2.0 * top
    for k in range(PRIOR):
        inner = inner - top[:, k : k + 1] * top[k : k + 1, :]
    gram = low
    for k in range(PRIOR):
        gram = gram - low[:, k : k + 1] * inner[k : k + 1, :]
    lane = lax.broadcasted_iota(jnp.int32, (16, 128), 1)
    row = lax.broadcasted_iota(jnp.int32, (16, 128), 0)
    work = jnp.where(lane < NEW, pltpu.roll(gram, 128 - PRIOR, 1), 0.0)
    work = work + jnp.where(lane == row + 16, 1.0, 0.0)
    work = work + jnp.where((lane >= 32) & (lane < 32 + PRIOR), pltpu.roll(low, 32, 1), 0.0)
    for k in range(NEW):
        pivot = work[k : k + 1, k : k + 1]
        scaled = work[k : k + 1, :] / jnp.sqrt(pivot)
        column = work[:, k : k + 1] / pivot
        work = jnp.where(row > k, work - column * work[k : k + 1, :], jnp.where(row == k, scaled, work))
    upper = jnp.where((lane >= row) & (lane < NEW), work, 0.0)
    both = jnp.concatenate([pltpu.roll(top, 128 - PRIOR, 1), upper], axis=0)
    both = jnp.concatenate([both, jnp.zeros((104, 128), jnp.float32)], axis=0)
    coeffs_ref[...] = both.T[:NEW, :FIELDS]
    for i in range(FIELDS):
        at = 16 + i if i < NEW else 32 + i - NEW
        spread[i] = jnp.broadcast_to(work[:, at : at + 1], (16, 128))

    stores = []
    for k in range(chunks):
        def some(g, carry, k=k):
            x, y = k * part + g // (wy // 16), g % (wy // 16)
            ys = pl.ds(pl.multiple_of(y * 16, 16), 16)
            inner = pl.ds(pl.multiple_of(H + y * 16, 8), 16)
            tiles = [fields[i][H + x, inner, :] for i in range(NEW)]
            tiles += [prior_ref[i, x, ys, :] for i in range(PRIOR)]
            for j in range(NEW):
                r = spread[0, j : j + 1, :] * tiles[0]
                for i in range(1, j + 1):
                    r = r + spread[i, j : j + 1, :] * tiles[i]
                for i in range(NEW, FIELDS):
                    r = r - spread[i, j : j + 1, :] * tiles[i]
                new[j, x, ys, :] = r
            return carry

        lax.fori_loop(0, part * (wy // 16), some, 0, unroll=2)
        xs = pl.ds(k * part, part)
        stores.append(pltpu.make_async_copy(new.at[:, xs], new_hbm.at[:, xs], out_sems.at[k]))
        stores[-1].start()
    for c in stores:
        c.wait()


def on_device(start, velocity, prior, shifts):
    wx, wy, wz = start.shape
    nx, ny = lax.axis_size("gx"), lax.axis_size("gy")
    devices = nx * ny
    swaps = {
        axis: [[pair for i in range(odd, n - 1, 2) for pair in ((i, i + 1), (i + 1, i))] for odd in (0, 1)]
        for axis, n in (("gx", nx), ("gy", ny))
    }
    ix, iy = lax.axis_index("gx"), lax.axis_index("gy")
    place = jnp.stack([ix > 0, ix < nx - 1, iy > 0, iy < ny - 1, ix % 2 == 1, iy % 2 == 1]).astype(jnp.int32)

    f32 = jnp.float32
    vmem = pl.BlockSpec(memory_space=pltpu.VMEM)
    smem = pl.BlockSpec(memory_space=pltpu.SMEM)
    hbm = pl.BlockSpec(memory_space=pl.ANY)
    limit = pltpu.CompilerParams(vmem_limit_bytes=12 * 1024 * 1024)
    edge_y = jax.ShapeDtypeStruct((4, wx, H, wz), f32)
    edge_x = jax.ShapeDtypeStruct((4, H, wy, wz), f32)
    corner = jax.ShapeDtypeStruct((CORNER, wz), f32)
    start_hbm, velocity_hbm, prior_hbm = (
        pltpu.with_memory_space_constraint(v, pltpu.HBM) for v in (start, velocity, prior)
    )
    y_even, y_odd, x_even, x_odd = pl.pallas_call(
        pack_kernel,
        out_shape=(edge_y, edge_y, edge_x, edge_x),
        in_specs=[smem, hbm, hbm],
        out_specs=(vmem,) * 4,
        scratch_shapes=[pltpu.SemaphoreType.DMA((8,))],
        compiler_params=limit,
        name="pack",
    )(place, start_hbm, velocity_hbm)
    xo = lax.ppermute(x_odd, "gx", swaps["gx"][1])
    xe = lax.ppermute(x_even, "gx", swaps["gx"][0])
    yo = lax.ppermute(y_odd, "gy", swaps["gy"][1])
    ye = lax.ppermute(y_even, "gy", swaps["gy"][0])
    ex, ey = wx + 2 * H, wy + 2 * H
    field = pltpu.VMEM((ex, ey, wz), f32)
    flow = pltpu.VMEM((3, ex, wy, wz), f32)
    strip = pltpu.VMEM((4, ex, 2 * H, wz), f32)
    early, prior_in, first, flows = pl.pallas_call(
        early_kernel,
        out_shape=(
            jax.ShapeDtypeStruct((len(EARLY), 8, 128), f32),
            pltpu.VMEM(prior.shape, f32),
            field,
            flow,
        ),
        in_specs=[hbm] * 3,
        out_specs=(vmem,) * 4,
        scratch_shapes=[pltpu.SemaphoreType.DMA((9, 2))],
        compiler_params=limit,
        name="early",
    )(prior_hbm, start_hbm, velocity_hbm)
    xe, xo, early = lax.optimization_barrier((xe, xo, early))
    c_even, c_odd = pl.pallas_call(
        corner_kernel,
        out_shape=(corner, corner),
        in_specs=[smem, vmem, vmem],
        out_specs=(vmem, vmem),
        compiler_params=limit,
        name="corner",
    )(place, xe, xo)
    co = lax.ppermute(c_odd, "gy", swaps["gy"][1])
    ce = lax.ppermute(c_even, "gy", swaps["gy"][0])
    *fields, flows, low, high, acc = pl.pallas_call(
        inner_kernel,
        out_shape=(*[field] * NEW, flow, strip, strip, pltpu.VMEM((SLOTS * 8, 128), f32)),
        in_specs=[smem, smem, hbm, hbm] + [vmem] * 4,
        out_specs=(vmem,) * (NEW + 4),
        scratch_shapes=[pltpu.VMEM((4, ex, wy, wz), f32), pltpu.SemaphoreType.DMA((4,))],
        input_output_aliases={6: 0, 7: NEW},
        compiler_params=limit,
        name="inner",
    )(shifts, place, xe, xo, prior_in, early, first, flows)
    low, high, *fields, sums = pl.pallas_call(
        outer_kernel,
        out_shape=(strip, strip, *[field] * NEW, jax.ShapeDtypeStruct((8, 128), f32)),
        in_specs=[smem, smem, hbm, hbm] + [vmem] * (6 + NEW),
        out_specs=(vmem,) * (NEW + 3),
        scratch_shapes=[
            pltpu.VMEM((3, ex, 2 * H, wz), f32),
            pltpu.VMEM((SLOTS * 8, 128), f32),
            pltpu.SemaphoreType.DMA((4,)),
        ],
        input_output_aliases={8 + k: k for k in range(NEW + 2)},
        compiler_params=limit,
        name="outer",
    )(shifts, place, yo, ye, co, ce, prior_in, acc, low, high, *fields)
    sums = sums + lax.ppermute(sums, "gx", swaps["gx"][0])
    chips = devices // 2
    cores = [[x * ny + y for x in range(core, nx, 2) for y in range(ny)] for core in (0, 1)]
    sums = jnp.broadcast_to(sums[None], (chips // 4, 8, 128)).reshape(chips * 2, 128)
    every = lax.all_to_all(sums, AXES, 0, 0, tiled=True, axis_index_groups=cores)
    chunks = 8
    first, second = pair_tables()
    basis_new, coeffs = pl.pallas_call(
        functools.partial(combine_kernel, float(devices * wx * wy * wz), chunks),
        out_shape=(
            jax.ShapeDtypeStruct((NEW, wx, wy, wz), f32),
            jax.ShapeDtypeStruct((NEW, FIELDS), f32),
        ),
        in_specs=[vmem] * (4 + NEW),
        out_specs=(hbm, vmem),
        scratch_shapes=[
            pltpu.VMEM((NEW, wx, wy, wz), f32),
            pltpu.VMEM((FIELDS, 16, 128), f32),
            pltpu.SemaphoreType.DMA((chunks,)),
        ],
        compiler_params=limit,
        name="combine",
    )(every, jnp.asarray(first), jnp.asarray(second), prior_in, *fields)
    return basis_new, coeffs.T


def solution(mesh):
    return jax.shard_map(
        on_device,
        mesh=mesh,
        in_specs=(P("gx", "gy", None), P(None, "gx", "gy", None), P(None, "gx", "gy", None), P()),
        out_specs=(P(None, "gx", "gy", None), P()),
        check_vma=False,
    )
```

time: 83.4 us -> 69.8 us (0.84)
  blocking collectives: 32.2 us -> 25.7 us
  waiting for transfers between devices: 7.14 us -> 2.97 us
  starting transfers between devices: 15.4 us -> 12.1 us
    all_to_all x1, blocking collectives: 32.2 us -> 25.7 us  [on_device(): lax.all_to_all(sums, AXES, 0, 0, tiled=True, axis_index_groups=cores)]
    ppermute x6 -> x7, waiting for transfers between devices: 7.14 us -> 2.97 us  [the longest x1 1.81 us: on_device(): xo = lax.ppermute(x_odd, 'gx', swaps['gx'][1])]
    ppermute x6 -> x7, starting transfers between devices: 15.4 us -> 12.1 us  [the longest x1 3.33 us: on_device(): xe = lax.ppermute(x_even, 'gx', swaps['gx'][0])]
    pallas_call x2 -> x3, Pallas kernels: 14.6 us -> 14.8 us  [the longest x1 7.42 us: on_device(): pl.pallas_call(inner_kernel, out_shape=(*[field] * NEW, flow, strip, stri...]
  transfers between devices with their start and end apart: 6 -> 7, of which waited for: 3 -> 2; matrix products, arithmetic and copies ran while one was open for 0% -> 0% of each run, Pallas kernels for 5% -> 16%
where the time goes in v2:
time: 69.8 us; the launch traced here: 69.6 us
  Pallas kernels  27.8 us (40%)
  blocking collectives  25.7 us (37%)
  starting transfers between devices  12.1 us (17%)
  waiting for transfers between devices  2.97 us (4%)
  between operations  0.8 us (1%)
    all_to_all x1, blocking collectives, on_device(): lax.all_to_all(sums, AXES, 0, 0, tiled=True, axis_index_groups=cores)  25.7 us
    pallas_call x1, Pallas kernels, on_device(): pl.pallas_call(functools.partial(combine_kernel, float(devices * wx * wy...  7.78 us
    pallas_call x1, Pallas kernels, on_device(): pl.pallas_call(inner_kernel, out_shape=(*[field] * NEW, flow, strip, stri...  7.42 us
    pallas_call x1, Pallas kernels, on_device(): pl.pallas_call(outer_kernel, out_shape=(strip, strip, *[field] * NEW, jax...  6.78 us
    ppermute x1, starting transfers between devices, on_device(): xe = lax.ppermute(x_even, 'gx', swaps['gx'][0])  3.33 us
    ppermute x1, starting transfers between devices, on_device(): ye = lax.ppermute(y_even, 'gy', swaps['gy'][0])  3.27 us
    pallas_call x1, Pallas kernels, on_device(): pl.pallas_call(early_kernel, out_shape=(jax.ShapeDtypeStruct((len(EARLY),...  3.06 us
    ppermute x1, starting transfers between devices, on_device(): ce = lax.ppermute(c_even, 'gy', swaps['gy'][0])  2.19 us
  transfers between devices with their start and end apart: 7, of which 2 were waited for; matrix products, arithmetic and copies ran while one was open for 0% of the time, Pallas kernels for 16%

profile of v2, /device:TPU:1, one launch (start us, length us, event | category | flops | bytes accessed | tf_op | source)
XLA Modules:
  0.0 69.6 jit_solution(10148520899811919152)
XLA Ops:
  0.7 0.1 stack.27
  0.8 2.2 %pack.1 = (f32[4,32,8,128]{3,2,1,0:T(8,128)S(1)}, f32[4,32,8,128]{3,2,1,0:T(8,128)S(1)}, f32[4,8,32,128]{3,2,1,0:T(8,128)S(1)}, f32[4,8,32,128]{3,2,1,0:T(8,128)S(1)}) custom-call(s32[6]{0:T(128)S(1)} %convert_element_type.3.place_ref, f32[32,32,128]{2,1,0:T(8,128)} %start_hbm.1, f32[3,32,32,128]{3,2,1,0:T(8,128)} %vel_hbm.1), custom_call_target="tpu_custom_call" | custom-call | tf_op jit(solution)/shard_map/pack/pallas_call | solution.py:412
  2.9 3.3 %collective-permute-start.2 = (f32[4,8,32,128]{3,2,1,0:T(8,128)S(1)}, f32[4,8,32,128]{3,2,1,0:T(8,128)S(1)}, u32[]{:S(2)}, u32[]{:S(2)}) collective-permute-start(f32[4,8,32,128]{3,2,1,0:T(8,128)S(1)} %get-tuple-element.41), channel_id=1, source_target_pairs={{0,32},{32,0},{64,96},{96,64},{128,160},{160,128},{192,224},{224,1... | collective-permute-start | bytes 1572872 | tf_op jit(solution)/shard_map/ppermute | solution.py:422
  6.3 1.9 %collective-permute-start.3 = (f32[4,8,32,128]{3,2,1,0:T(8,128)S(1)}, f32[4,8,32,128]{3,2,1,0:T(8,128)S(1)}, u32[]{:S(2)}, u32[]{:S(2)}) collective-permute-start(f32[4,8,32,128]{3,2,1,0:T(8,128)S(1)} %get-tuple-element.42), channel_id=1, source_target_pairs={{32,64},{64,32},{96,128},{128,96},{160,192},{192,160},{33,65},{65,... | collective-permute-start | bytes 1572872 | tf_op jit(solution)/shard_map/ppermute | solution.py:421
  8.2 0.7 collective-permute-start
  8.9 0.0 copy-start.2
  8.9 3.3 %collective-permute-start.1 = (f32[4,32,8,128]{3,2,1,0:T(8,128)S(1)}, f32[4,32,8,128]{3,2,1,0:T(8,128)S(1)}, u32[]{:S(2)}, u32[]{:S(2)}) collective-permute-start(f32[4,32,8,128]{3,2,1,0:T(8,128)S(1)} %get-tuple-element.40), channel_id=1, source_target_pairs={{0,1},{1,0},{2,3},{3,2},{4,5},{5,4},{6,7},{7,6},{8,9},{9,8},{10,11... | collective-permute-start | bytes 1572872 | tf_op jit(solution)/shard_map/ppermute | solution.py:424
  12.2 3.1 %early.1 = (f32[45,8,128]{2,1,0:T(8,128)S(1)}, f32[8,32,32,128]{3,2,1,0:T(8,128)S(1)}, f32[48,48,128]{2,1,0:T(8,128)S(1)}, f32[3,48,32,128]{3,2,1,0:T(8,128)S(1)}) custom-call(f32[8,32,32,128]{3,2,1,0:T(8,128)} %prior_hbm.1, f32[32,32,128]{2,1,0:T(8,128)} %start_hbm.1, f32[3,32,32,128]{3,2,1,0:T(8,128)} %vel_hbm.1), custom_call_target="tpu_custom_call" | custom-call | tf_op jit(solution)/shard_map/early/pallas_call | solution.py:429
  15.2 0.0 collective-permute-done.2.xe_ref
  15.2 1.8 %collective-permute-done.3.xo_ref = f32[4,8,32,128]{3,2,1,0:T(8,128)S(1)} collective-permute-done((f32[4,8,32,128]{3,2,1,0:T(8,128)S(1)}, f32[4,8,32,128]{3,2,1,0:T(8,128)S(1)}, u32[]{:S(2)}, u32[]{:S(2)}) %collective-permute-start.3) | collective-permute-done | bytes 524320 | tf_op jit(solution)/shard_map/ppermute | solution.py:421
  17.1 0.6 corner.1
  17.7 0.7 collective-permute-start.4
  18.3 2.2 %collective-permute-start.5 = (f32[182,128]{1,0:T(8,128)S(1)}, f32[182,128]{1,0:T(8,128)S(1)}, u32[]{:S(2)}, u32[]{:S(2)}) collective-permute-start(f32[182,128]{1,0:T(8,128)S(1)} %get-tuple-element.47), channel_id=1, source_target_pairs={{0,1},{1,0},{2,3},{3,2},{4,5},{5,4},{6,7},{7,6},{8,9},{9,8},{10,11... | collective-permute-start | bytes 279560 | tf_op jit(solution)/shard_map/ppermute | solution.py:453
  20.5 0.0 copy-done.2
  20.5 7.4 %inner.1 = (f32[48,48,128]{2,1,0:T(8,128)S(1)}, f32[48,48,128]{2,1,0:T(8,128)S(1)}, f32[48,48,128]{2,1,0:T(8,128)S(1)}, f32[48,48,128]{2,1,0:T(8,128)S(1)}, f32[...) custom-call(f32[8]{0:T(128)S(1)} %copy-done.2, ...), custom_call_target="tpu_custom_call", output_to_operand_aliasing={{0}: (6, {}), {9}: (7, {})} | custom-call | tf_op jit(solution)/shard_map/inner/pallas_call | solution.py:454
  28.0 0.0 collective-permute-done.yo_ref
  28.0 0.0 collective-permute-done.1.ye_ref
  28.0 0.0 collective-permute-done.4.co_ref
  28.0 0.0 collective-permute-done.5.ce_ref
  28.0 0.0 copy-start
  28.0 0.0 copy-start.1
  28.0 6.8 %outer.1 = (f32[4,48,16,128]{3,2,1,0:T(8,128)S(1)}, f32[4,48,16,128]{3,2,1,0:T(8,128)S(1)}, f32[48,48,128]{2,1,0:T(8,128)S(1)}, f32[48,48,128]{2,1,0:T(8,128)S(1...) custom-call(f32[8]{0:T(128)S(1)} %copy-done.2, ...), custom_call_target="tpu_custom_call", output_to_operand_aliasing={{0}: (8, {}), {1}: (9, {}), {2}: (10, {}), {3}: (11, {}), {... | custom-call | tf_op jit(solution)/shard_map/outer/pallas_call | solution.py:464
  34.8 0.1 collective-permute-start.6
  34.9 1.2 %collective-permute-done.6 = f32[8,128]{1,0:T(8,128)S(1)} collective-permute-done((f32[8,128]{1,0:T(8,128)S(1)}, f32[8,128]{1,0:T(8,128)S(1)}, u32[]{:S(2)}, u32[]{:S(2)}) %collective-permute-start.6) | collective-permute-done | bytes 4128 | tf_op jit(solution)/shard_map/ppermute | solution.py:478
  36.1 25.7 %all_to_all.11 = f32[128,2,128]{2,1,0:T(2,128)S(1)} all-to-all(f32[128,2,128]{2,1,0:T(2,128)S(1)} %bitcast.10), channel_id=1, replica_groups={{0,1,2,3,4,5,6,7,8,9,10,11,12,13,14,15,16,17,18,19,20,21,22,23,24,25,26..., dimensions={0} | all-to-all | bytes 262144 | tf_op jit(solution)/shard_map/all_to_all | solution.py:482
  61.8 0.0 copy-done
  61.8 0.0 copy-done.1
  61.8 7.8 %combine.1 = (f32[9,32,32,128]{3,2,1,0:T(8,128)}, f32[9,17]{1,0:T(8,128)}) custom-call(f32[256,128]{1,0:T(8,128)S(1)} %bitcast.9, f32[128,256]{1,0:T(8,128)S(1)} %copy-done.1, f32[128,256]{1,0:T(8,128)S(1)} %copy-done, f32[8,32,32,128]{3,2,1,0:T(8,128)S(1)} %get-tuple-element.48.prior_ref, f32[48,48,128]{2,1,0:T(8,128)S(1)} %get-tuple-element.65.rest_0_, ...), custom_call_target="tpu_custom_call" | custom-call | tf_op jit(solution)/shard_map/combine/pallas_call | solution.py:485
  (3 shorter events, 0.0 us)
Async XLA Ops:
  2.9 12.3 %collective-permute-start.2 = (f32[4,8,32,128]{3,2,1,0:T(8,128)S(1)}, f32[4,8,32,128]{3,2,1,0:T(8,128)S(1)}, u32[]{:S(2)}, u32[]{:S(2)}) collective-permute-start(f32[4,8,32,128]{3,2,1,0:T(8,128)S(1)} %get-tuple-element.41), channel_id=1, source_target_pairs={{0,32},{32,0},{64,96},{96,64},{128,160},{160,128},{192,224},{224,1... | collective-permute-start | bytes 1572872 | tf_op jit(solution)/shard_map/ppermute | solution.py:422
  6.3 10.8 %collective-permute-start.3 = (f32[4,8,32,128]{3,2,1,0:T(8,128)S(1)}, f32[4,8,32,128]{3,2,1,0:T(8,128)S(1)}, u32[]{:S(2)}, u32[]{:S(2)}) collective-permute-start(f32[4,8,32,128]{3,2,1,0:T(8,128)S(1)} %get-tuple-element.42), channel_id=1, source_target_pairs={{32,64},{64,32},{96,128},{128,96},{160,192},{192,160},{33,65},{65,... | collective-permute-start | bytes 1572872 | tf_op jit(solution)/shard_map/ppermute | solution.py:421
  8.2 19.8 %collective-permute-start = (f32[4,32,8,128]{3,2,1,0:T(8,128)S(1)}, f32[4,32,8,128]{3,2,1,0:T(8,128)S(1)}, u32[]{:S(2)}, u32[]{:S(2)}) collective-permute-start(f32[4,32,8,128]{3,2,1,0:T(8,128)S(1)} %get-tuple-element.39), channel_id=1, source_target_pairs={{1,2},{2,1},{3,4},{4,3},{5,6},{6,5},{7,8},{8,7},{9,10},{10,9},{11,... | collective-permute-start | bytes 1572872 | tf_op jit(solution)/shard_map/ppermute | solution.py:423
  8.9 11.6 %copy-start.2 = (f32[8]{0:T(128)S(1)}, f32[8]{0:T(128)}, u32[]{:S(2)}) copy-start(f32[8]{0:T(128)} %shifts_ref.3) | copy-start | bytes 100
  8.9 19.1 %collective-permute-start.1 = (f32[4,32,8,128]{3,2,1,0:T(8,128)S(1)}, f32[4,32,8,128]{3,2,1,0:T(8,128)S(1)}, u32[]{:S(2)}, u32[]{:S(2)}) collective-permute-start(f32[4,32,8,128]{3,2,1,0:T(8,128)S(1)} %get-tuple-element.40), channel_id=1, source_target_pairs={{0,1},{1,0},{2,3},{3,2},{4,5},{5,4},{6,7},{7,6},{8,9},{9,8},{10,11... | collective-permute-start | bytes 1572872 | tf_op jit(solution)/shard_map/ppermute | solution.py:424
  17.7 10.3 %collective-permute-start.4 = (f32[182,128]{1,0:T(8,128)S(1)}, f32[182,128]{1,0:T(8,128)S(1)}, u32[]{:S(2)}, u32[]{:S(2)}) collective-permute-start(f32[182,128]{1,0:T(8,128)S(1)} %get-tuple-element.46), channel_id=1, source_target_pairs={{1,2},{2,1},{3,4},{4,3},{5,6},{6,5},{7,8},{8,7},{9,10},{10,9},{11,... | collective-permute-start | bytes 279560 | tf_op jit(solution)/shard_map/ppermute | solution.py:452
  18.3 9.7 %collective-permute-start.5 = (f32[182,128]{1,0:T(8,128)S(1)}, f32[182,128]{1,0:T(8,128)S(1)}, u32[]{:S(2)}, u32[]{:S(2)}) collective-permute-start(f32[182,128]{1,0:T(8,128)S(1)} %get-tuple-element.47), channel_id=1, source_target_pairs={{0,1},{1,0},{2,3},{3,2},{4,5},{5,4},{6,7},{7,6},{8,9},{9,8},{10,11... | collective-permute-start | bytes 279560 | tf_op jit(solution)/shard_map/ppermute | solution.py:453
  28.0 33.8 %copy-start = (f32[128,256]{1,0:T(8,128)S(1)}, f32[128,256]{1,0:T(8,128)}, u32[]{:S(2)}) copy-start(f32[128,256]{1,0:T(8,128)} %constant.37.clone.second_ref) | copy-start | bytes 393220
  28.0 33.8 %copy-start.1 = (f32[128,256]{1,0:T(8,128)S(1)}, f32[128,256]{1,0:T(8,128)}, u32[]{:S(2)}) copy-start(f32[128,256]{1,0:T(8,128)} %constant.36.clone.first_ref) | copy-start | bytes 393220
  34.8 1.3 %collective-permute-start.6 = (f32[8,128]{1,0:T(8,128)S(1)}, f32[8,128]{1,0:T(8,128)S(1)}, u32[]{:S(2)}, u32[]{:S(2)}) collective-permute-start(f32[8,128]{1,0:T(8,128)S(1)} %get-tuple-element.64), channel_id=1, source_target_pairs={{0,32},{32,0},{64,96},{96,64},{128,160},{160,128},{192,224},{224,1... | collective-permute-start | bytes 12296 | tf_op jit(solution)/shard_map/ppermute | solution.py:478

commit v3 on v2

--- a/solution.py
+++ b/solution.py
@@ -87,6 +87,13 @@
         put(at + CORNER // 2, f, d - 1, n, False)
 
 
+def thirds(a):
+    high = a.astype(jnp.bfloat16).astype(jnp.float32)
+    rest = a - high
+    middle = rest.astype(jnp.bfloat16).astype(jnp.float32)
+    return high, middle, rest - middle
+
+
 def products(load, pairs, groups, start=None):
     used = sorted({f for pair in pairs for f in pair})
 
@@ -96,7 +103,7 @@
 
     if start is None:
         start = (jnp.zeros((8, 128), jnp.float32),) * len(pairs)
-    return lax.fori_loop(0, groups, body, start, unroll=8)
+    return lax.fori_loop(0, groups, body, start, unroll=16)
 
 
 def early_kernel(prior_hbm, start_hbm, vel_hbm, out_ref, prior_ref, field, flow, sems):
@@ -310,8 +317,8 @@
     for s in range(1, 8):
         by_lane = by_lane + acc[pl.ds(s, SLOTS, stride=8), :]
     total = lax.dot_general(
-        jnp.ones((8, 128), jnp.float32), by_lane, (((1,), (1,)), ((), ())),
-        precision=lax.Precision.HIGHEST, preferred_element_type=jnp.float32,
+        jnp.ones((8, 3 * 128), jnp.float32), jnp.concatenate(thirds(by_lane), axis=1), (((1,), (1,)), ((), ())),
+        preferred_element_type=jnp.float32,
     )
     second = jnp.concatenate([total[:, 128:], jnp.zeros((8, 256 - SLOTS), jnp.float32)], axis=1)
     even = lax.broadcasted_iota(jnp.int32, (8, 128), 0) % 2 == 0
@@ -331,12 +338,14 @@
     total = total + pltpu.roll(total, 4, 0)
     total = (total + pltpu.roll(total, 2, 0)) * (1.0 / count)
     flat = jnp.concatenate([total[0:1, :], total[1:2, :]], axis=1)
-    contract = functools.partial(
-        lax.dot_general, dimension_numbers=(((1,), (1,)), ((), ())),
-        precision=lax.Precision.HIGHEST, preferred_element_type=jnp.float32,
-    )
-    first, second = first_ref[...], second_ref[...]
-    full = contract(first[:24] * flat, second) + contract(second[:24] * flat, first)
+    first, second = first_ref[:24], second_ref[:24]
+
+    def contract(left, right):
+        rows = jnp.concatenate([left * part_of for part_of in thirds(flat)], axis=0)
+        r = lax.dot_general(rows, right[...], (((1,), (1,)), ((), ())), preferred_element_type=jnp.float32)
+        return (r[:24] + r[24:48]) + r[48:]
+
+    full = contract(first, second_ref) + contract(second, first_ref)
     top, low = full[0:8, :], full[8:24, :]
     inner = 2.0 * top
     for k in range(PRIOR):
@@ -346,22 +355,24 @@
         gram = gram - low[:, k : k + 1] * inner[k : k + 1, :]
     lane = lax.broadcasted_iota(jnp.int32, (16, 128), 1)
     row = lax.broadcasted_iota(jnp.int32, (16, 128), 0)
-    work = jnp.where(lane < NEW, pltpu.roll(gram, 128 - PRIOR, 1), 0.0)
-    work = work + jnp.where(lane == row + 16, 1.0, 0.0)
-    work = work + jnp.where((lane >= 32) & (lane < 32 + PRIOR), pltpu.roll(low, 32, 1), 0.0)
+    columns = [jnp.broadcast_to(gram[:, PRIOR + k : PRIOR + k + 1], (16, 128)) for k in range(NEW)]
+    units = [jnp.where(row == k, 1.0, 0.0) for k in range(NEW)]
+    coefs = [jnp.broadcast_to(low[:, k : k + 1], (16, 128)) for k in range(PRIOR)]
+    pivots = jnp.ones((16, 128), jnp.float32)
     for k in range(NEW):
-        pivot = work[k : k + 1, k : k + 1]
-        scaled = work[k : k + 1, :] / jnp.sqrt(pivot)
-        column = work[:, k : k + 1] / pivot
-        work = jnp.where(row > k, work - column * work[k : k + 1, :], jnp.where(row == k, scaled, work))
-    upper = jnp.where((lane >= row) & (lane < NEW), work, 0.0)
+        pivot = columns[k][k : k + 1, :]
+        pivots = jnp.where(row == k, pivot, pivots)
+        factor = jnp.where(row > k, columns[k] * (1.0 / pivot), 0.0)
+        columns[k + 1 :] = [c - factor * c[k : k + 1, :] for c in columns[k + 1 :]]
+        units[: k + 1] = [c - factor * c[k : k + 1, :] for c in units[: k + 1]]
+        coefs = [c - factor * c[k : k + 1, :] for c in coefs]
+    scale = 1.0 / jnp.sqrt(pivots)
+    for i, c in enumerate(units + coefs):
+        spread[i] = c * scale
+    upper = jnp.zeros((16, 128), jnp.float32)
+    for k in range(NEW):
+        upper = jnp.where((lane == k) & (row <= k), columns[k] * scale, upper)
     both = jnp.concatenate([pltpu.roll(top, 128 - PRIOR, 1), upper], axis=0)
-    both = jnp.concatenate([both, jnp.zeros((104, 128), jnp.float32)], axis=0)
-    coeffs_ref[...] = both.T[:NEW, :FIELDS]
-    for i in range(FIELDS):
-        at = 16 + i if i < NEW else 32 + i - NEW
-        spread[i] = jnp.broadcast_to(work[:, at : at + 1], (16, 128))
-
     stores = []
     for k in range(chunks):
         def some(g, carry, k=k):
@@ -383,6 +394,8 @@
         xs = pl.ds(k * part, part)
         stores.append(pltpu.make_async_copy(new.at[:, xs], new_hbm.at[:, xs], out_sems.at[k]))
         stores[-1].start()
+    both = jnp.concatenate([both, jnp.zeros((104, 128), jnp.float32)], axis=0)
+    coeffs_ref[...] = both.T[:NEW, :FIELDS]
     for c in stores:
         c.wait()
 

time: 69.8 us -> 68.4 us (0.980)
  Pallas kernels: 27.8 us -> 26.5 us
    pallas_call x1, Pallas kernels: 7.78 us -> 6.96 us  [on_device(): pl.pallas_call(functools.partial(combine_kernel, float(devices * wx * wy...]
where the time goes in v3:
time: 68.4 us; the launch traced here: 68.2 us
  Pallas kernels  26.5 us (39%)
  blocking collectives  25.6 us (37%)
  starting transfers between devices  12.1 us (18%)
  waiting for transfers between devices  3.03 us (4%)
  between operations  0.8 us (1%)
    all_to_all x1, blocking collectives, on_device(): lax.all_to_all(sums, AXES, 0, 0, tiled=True, axis_index_groups=cores)  25.6 us
    pallas_call x1, Pallas kernels, on_device(): pl.pallas_call(inner_kernel, out_shape=(*[field] * NEW, flow, strip, stri...  7.22 us
    pallas_call x1, Pallas kernels, on_device(): pl.pallas_call(functools.partial(combine_kernel, float(devices * wx * wy...  6.96 us
    pallas_call x1, Pallas kernels, on_device(): pl.pallas_call(outer_kernel, out_shape=(strip, strip, *[field] * NEW, jax...  6.51 us
    ppermute x1, starting transfers between devices, on_device(): xe = lax.ppermute(x_even, 'gx', swaps['gx'][0])  3.33 us
    ppermute x1, starting transfers between devices, on_device(): ye = lax.ppermute(y_even, 'gy', swaps['gy'][0])  3.27 us
    pallas_call x1, Pallas kernels, on_device(): pl.pallas_call(early_kernel, out_shape=(jax.ShapeDtypeStruct((len(EARLY),...  3 us
    ppermute x1, starting transfers between devices, on_device(): ce = lax.ppermute(c_even, 'gy', swaps['gy'][0])  2.19 us
  transfers between devices with their start and end apart: 7, of which 2 were waited for; matrix products, arithmetic and copies ran while one was open for 0% of the time, Pallas kernels for 16%

profile of v3, /device:TPU:1, one launch (start us, length us, event | category | flops | bytes accessed | tf_op | source)
XLA Modules:
  0.0 68.2 jit_solution(2071444560294888350)
XLA Ops:
  0.7 0.1 stack.27
  0.8 2.2 %pack.1 = (f32[4,32,8,128]{3,2,1,0:T(8,128)S(1)}, f32[4,32,8,128]{3,2,1,0:T(8,128)S(1)}, f32[4,8,32,128]{3,2,1,0:T(8,128)S(1)}, f32[4,8,32,128]{3,2,1,0:T(8,128)S(1)}) custom-call(s32[6]{0:T(128)S(1)} %convert_element_type.3.place_ref, f32[32,32,128]{2,1,0:T(8,128)} %start_hbm.1, f32[3,32,32,128]{3,2,1,0:T(8,128)} %vel_hbm.1), custom_call_target="tpu_custom_call" | custom-call | tf_op jit(solution)/shard_map/pack/pallas_call | solution.py:425
  2.9 3.3 %collective-permute-start.2 = (f32[4,8,32,128]{3,2,1,0:T(8,128)S(1)}, f32[4,8,32,128]{3,2,1,0:T(8,128)S(1)}, u32[]{:S(2)}, u32[]{:S(2)}) collective-permute-start(f32[4,8,32,128]{3,2,1,0:T(8,128)S(1)} %get-tuple-element.41), channel_id=1, source_target_pairs={{0,32},{32,0},{64,96},{96,64},{128,160},{160,128},{192,224},{224,1... | collective-permute-start | bytes 1572872 | tf_op jit(solution)/shard_map/ppermute | solution.py:435
  6.3 1.9 %collective-permute-start.3 = (f32[4,8,32,128]{3,2,1,0:T(8,128)S(1)}, f32[4,8,32,128]{3,2,1,0:T(8,128)S(1)}, u32[]{:S(2)}, u32[]{:S(2)}) collective-permute-start(f32[4,8,32,128]{3,2,1,0:T(8,128)S(1)} %get-tuple-element.42), channel_id=1, source_target_pairs={{32,64},{64,32},{96,128},{128,96},{160,192},{192,160},{33,65},{65,... | collective-permute-start | bytes 1572872 | tf_op jit(solution)/shard_map/ppermute | solution.py:434
  8.2 0.7 %collective-permute-start = (f32[4,32,8,128]{3,2,1,0:T(8,128)S(1)}, f32[4,32,8,128]{3,2,1,0:T(8,128)S(1)}, u32[]{:S(2)}, u32[]{:S(2)}) collective-permute-start(f32[4,32,8,128]{3,2,1,0:T(8,128)S(1)} %get-tuple-element.39), channel_id=1, source_target_pairs={{1,2},{2,1},{3,4},{4,3},{5,6},{6,5},{7,8},{8,7},{9,10},{10,9},{11,... | collective-permute-start | bytes 1572872 | tf_op jit(solution)/shard_map/ppermute | solution.py:436
  8.9 0.0 copy-start.2
  8.9 3.3 %collective-permute-start.1 = (f32[4,32,8,128]{3,2,1,0:T(8,128)S(1)}, f32[4,32,8,128]{3,2,1,0:T(8,128)S(1)}, u32[]{:S(2)}, u32[]{:S(2)}) collective-permute-start(f32[4,32,8,128]{3,2,1,0:T(8,128)S(1)} %get-tuple-element.40), channel_id=1, source_target_pairs={{0,1},{1,0},{2,3},{3,2},{4,5},{5,4},{6,7},{7,6},{8,9},{9,8},{10,11... | collective-permute-start | bytes 1572872 | tf_op jit(solution)/shard_map/ppermute | solution.py:437
  12.2 3.0 %early.1 = (f32[45,8,128]{2,1,0:T(8,128)S(1)}, f32[8,32,32,128]{3,2,1,0:T(8,128)S(1)}, f32[48,48,128]{2,1,0:T(8,128)S(1)}, f32[3,48,32,128]{3,2,1,0:T(8,128)S(1)}) custom-call(f32[8,32,32,128]{3,2,1,0:T(8,128)} %prior_hbm.1, f32[32,32,128]{2,1,0:T(8,128)} %start_hbm.1, f32[3,32,32,128]{3,2,1,0:T(8,128)} %vel_hbm.1), custom_call_target="tpu_custom_call" | custom-call | tf_op jit(solution)/shard_map/early/pallas_call | solution.py:442
  15.2 0.0 collective-permute-done.2.xe_ref
  15.2 1.9 %collective-permute-done.3.xo_ref = f32[4,8,32,128]{3,2,1,0:T(8,128)S(1)} collective-permute-done((f32[4,8,32,128]{3,2,1,0:T(8,128)S(1)}, f32[4,8,32,128]{3,2,1,0:T(8,128)S(1)}, u32[]{:S(2)}, u32[]{:S(2)}) %collective-permute-start.3) | collective-permute-done | bytes 524320 | tf_op jit(solution)/shard_map/ppermute | solution.py:434
  17.1 0.6 corner.1
  17.7 0.7 collective-permute-start.4
  18.3 2.2 %collective-permute-start.5 = (f32[182,128]{1,0:T(8,128)S(1)}, f32[182,128]{1,0:T(8,128)S(1)}, u32[]{:S(2)}, u32[]{:S(2)}) collective-permute-start(f32[182,128]{1,0:T(8,128)S(1)} %get-tuple-element.47), channel_id=1, source_target_pairs={{0,1},{1,0},{2,3},{3,2},{4,5},{5,4},{6,7},{7,6},{8,9},{9,8},{10,11... | collective-permute-start | bytes 279560 | tf_op jit(solution)/shard_map/ppermute | solution.py:466
  20.5 0.0 copy-done.2
  20.5 7.2 %inner.1 = (f32[48,48,128]{2,1,0:T(8,128)S(1)}, f32[48,48,128]{2,1,0:T(8,128)S(1)}, f32[48,48,128]{2,1,0:T(8,128)S(1)}, f32[48,48,128]{2,1,0:T(8,128)S(1)}, f32[...) custom-call(f32[8]{0:T(128)S(1)} %copy-done.2, ...), custom_call_target="tpu_custom_call", output_to_operand_aliasing={{0}: (6, {}), {9}: (7, {})} | custom-call | tf_op jit(solution)/shard_map/inner/pallas_call | solution.py:467
  27.8 0.0 collective-permute-done.yo_ref
  27.8 0.0 collective-permute-done.1.ye_ref
  27.8 0.0 collective-permute-done.4.co_ref
  27.8 0.0 collective-permute-done.5.ce_ref
  27.8 0.0 copy-start
  27.8 0.0 copy-start.1
  27.8 6.5 %outer.1 = (f32[4,48,16,128]{3,2,1,0:T(8,128)S(1)}, f32[4,48,16,128]{3,2,1,0:T(8,128)S(1)}, f32[48,48,128]{2,1,0:T(8,128)S(1)}, f32[48,48,128]{2,1,0:T(8,128)S(1...) custom-call(f32[8]{0:T(128)S(1)} %copy-done.2, ...), custom_call_target="tpu_custom_call", output_to_operand_aliasing={{0}: (8, {}), {1}: (9, {}), {2}: (10, {}), {3}: (11, {}), {... | custom-call | tf_op jit(solution)/shard_map/outer/pallas_call | solution.py:477
  34.3 0.1 collective-permute-start.6
  34.4 1.2 %collective-permute-done.6 = f32[8,128]{1,0:T(8,128)S(1)} collective-permute-done((f32[8,128]{1,0:T(8,128)S(1)}, f32[8,128]{1,0:T(8,128)S(1)}, u32[]{:S(2)}, u32[]{:S(2)}) %collective-permute-start.6) | collective-permute-done | bytes 4128 | tf_op jit(solution)/shard_map/ppermute | solution.py:491
  35.6 25.6 %all_to_all.11 = f32[128,2,128]{2,1,0:T(2,128)S(1)} all-to-all(f32[128,2,128]{2,1,0:T(2,128)S(1)} %bitcast.10), channel_id=1, replica_groups={{0,1,2,3,4,5,6,7,8,9,10,11,12,13,14,15,16,17,18,19,20,21,22,23,24,25,26..., dimensions={0} | all-to-all | bytes 262144 | tf_op jit(solution)/shard_map/all_to_all | solution.py:495
  61.3 0.0 copy-done
  61.3 0.0 copy-done.1
  61.3 7.0 %combine.1 = (f32[9,32,32,128]{3,2,1,0:T(8,128)}, f32[9,17]{1,0:T(8,128)}) custom-call(f32[256,128]{1,0:T(8,128)S(1)} %bitcast.9, f32[128,256]{1,0:T(8,128)S(1)} %copy-done.1, f32[128,256]{1,0:T(8,128)S(1)} %copy-done, f32[8,32,32,128]{3,2,1,0:T(8,128)S(1)} %get-tuple-element.48.prior_ref, f32[48,48,128]{2,1,0:T(8,128)S(1)} %get-tuple-element.65.rest_0_, ...), custom_call_target="tpu_custom_call" | custom-call | tf_op jit(solution)/shard_map/combine/pallas_call | solution.py:498
  (3 shorter events, 0.0 us)
Async XLA Ops:
  2.9 12.2 %collective-permute-start.2 = (f32[4,8,32,128]{3,2,1,0:T(8,128)S(1)}, f32[4,8,32,128]{3,2,1,0:T(8,128)S(1)}, u32[]{:S(2)}, u32[]{:S(2)}) collective-permute-start(f32[4,8,32,128]{3,2,1,0:T(8,128)S(1)} %get-tuple-element.41), channel_id=1, source_target_pairs={{0,32},{32,0},{64,96},{96,64},{128,160},{160,128},{192,224},{224,1... | collective-permute-start | bytes 1572872 | tf_op jit(solution)/shard_map/ppermute | solution.py:435
  6.3 10.8 %collective-permute-start.3 = (f32[4,8,32,128]{3,2,1,0:T(8,128)S(1)}, f32[4,8,32,128]{3,2,1,0:T(8,128)S(1)}, u32[]{:S(2)}, u32[]{:S(2)}) collective-permute-start(f32[4,8,32,128]{3,2,1,0:T(8,128)S(1)} %get-tuple-element.42), channel_id=1, source_target_pairs={{32,64},{64,32},{96,128},{128,96},{160,192},{192,160},{33,65},{65,... | collective-permute-start | bytes 1572872 | tf_op jit(solution)/shard_map/ppermute | solution.py:434
  8.2 19.6 %collective-permute-start = (f32[4,32,8,128]{3,2,1,0:T(8,128)S(1)}, f32[4,32,8,128]{3,2,1,0:T(8,128)S(1)}, u32[]{:S(2)}, u32[]{:S(2)}) collective-permute-start(f32[4,32,8,128]{3,2,1,0:T(8,128)S(1)} %get-tuple-element.39), channel_id=1, source_target_pairs={{1,2},{2,1},{3,4},{4,3},{5,6},{6,5},{7,8},{8,7},{9,10},{10,9},{11,... | collective-permute-start | bytes 1572872 | tf_op jit(solution)/shard_map/ppermute | solution.py:436
  8.9 11.6 %copy-start.2 = (f32[8]{0:T(128)S(1)}, f32[8]{0:T(128)}, u32[]{:S(2)}) copy-start(f32[8]{0:T(128)} %shifts_ref.3) | copy-start | bytes 100
  8.9 18.9 %collective-permute-start.1 = (f32[4,32,8,128]{3,2,1,0:T(8,128)S(1)}, f32[4,32,8,128]{3,2,1,0:T(8,128)S(1)}, u32[]{:S(2)}, u32[]{:S(2)}) collective-permute-start(f32[4,32,8,128]{3,2,1,0:T(8,128)S(1)} %get-tuple-element.40), channel_id=1, source_target_pairs={{0,1},{1,0},{2,3},{3,2},{4,5},{5,4},{6,7},{7,6},{8,9},{9,8},{10,11... | collective-permute-start | bytes 1572872 | tf_op jit(solution)/shard_map/ppermute | solution.py:437
  17.7 10.1 %collective-permute-start.4 = (f32[182,128]{1,0:T(8,128)S(1)}, f32[182,128]{1,0:T(8,128)S(1)}, u32[]{:S(2)}, u32[]{:S(2)}) collective-permute-start(f32[182,128]{1,0:T(8,128)S(1)} %get-tuple-element.46), channel_id=1, source_target_pairs={{1,2},{2,1},{3,4},{4,3},{5,6},{6,5},{7,8},{8,7},{9,10},{10,9},{11,... | collective-permute-start | bytes 279560 | tf_op jit(solution)/shard_map/ppermute | solution.py:465
  18.3 9.5 %collective-permute-start.5 = (f32[182,128]{1,0:T(8,128)S(1)}, f32[182,128]{1,0:T(8,128)S(1)}, u32[]{:S(2)}, u32[]{:S(2)}) collective-permute-start(f32[182,128]{1,0:T(8,128)S(1)} %get-tuple-element.47), channel_id=1, source_target_pairs={{0,1},{1,0},{2,3},{3,2},{4,5},{5,4},{6,7},{7,6},{8,9},{9,8},{10,11... | collective-permute-start | bytes 279560 | tf_op jit(solution)/shard_map/ppermute | solution.py:466
  27.8 33.5 %copy-start = (f32[128,256]{1,0:T(8,128)S(1)}, f32[128,256]{1,0:T(8,128)}, u32[]{:S(2)}) copy-start(f32[128,256]{1,0:T(8,128)} %constant.37.clone.second_ref) | copy-start | bytes 393220
  27.8 33.4 %copy-start.1 = (f32[128,256]{1,0:T(8,128)S(1)}, f32[128,256]{1,0:T(8,128)}, u32[]{:S(2)}) copy-start(f32[128,256]{1,0:T(8,128)} %constant.36.clone.first_ref) | copy-start | bytes 393220
  34.3 1.3 %collective-permute-start.6 = (f32[8,128]{1,0:T(8,128)S(1)}, f32[8,128]{1,0:T(8,128)S(1)}, u32[]{:S(2)}, u32[]{:S(2)}) collective-permute-start(f32[8,128]{1,0:T(8,128)S(1)} %get-tuple-element.64), channel_id=1, source_target_pairs={{0,32},{32,0},{64,96},{96,64},{128,160},{160,128},{192,224},{224,1... | collective-permute-start | bytes 12296 | tf_op jit(solution)/shard_map/ppermute | solution.py:491

commit v4 on v3

--- a/solution.py
+++ b/solution.py
@@ -183,7 +183,7 @@
         rows(H - halo + k, n, scale_low)
         rows(H + wx + k, n, scale_high)
     if not ready:
-        lax.fori_loop(0, wx // 16, some(16), 0)
+        some(wx)(0, 0)
 
 
 def late_products(fields, prior_ref, wx, blocks, acc, start):

time: 68.4 us -> 67.7 us (0.990)
  Pallas kernels: 26.5 us -> 25.5 us
    pallas_call x1, Pallas kernels: 6.51 us -> 5.68 us  [on_device(): pl.pallas_call(outer_kernel, out_shape=(strip, strip, *[field] * NEW, jax...]
where the time goes in v4:
time: 67.7 us; the launch traced here: 67.5 us
  blocking collectives  25.7 us (38%)
  Pallas kernels  25.5 us (38%)
  starting transfers between devices  12.1 us (18%)
  waiting for transfers between devices  3.03 us (4%)
  between operations  0.96 us (1%)
    all_to_all x1, blocking collectives, on_device(): lax.all_to_all(sums, AXES, 0, 0, tiled=True, axis_index_groups=cores)  25.7 us
    pallas_call x1, Pallas kernels, on_device(): pl.pallas_call(inner_kernel, out_shape=(*[field] * NEW, flow, strip, stri...  7.1 us
    pallas_call x1, Pallas kernels, on_device(): pl.pallas_call(functools.partial(combine_kernel, float(devices * wx * wy...  6.96 us
    pallas_call x1, Pallas kernels, on_device(): pl.pallas_call(outer_kernel, out_shape=(strip, strip, *[field] * NEW, jax...  5.68 us
    ppermute x1, starting transfers between devices, on_device(): xe = lax.ppermute(x_even, 'gx', swaps['gx'][0])  3.33 us
    ppermute x1, starting transfers between devices, on_device(): ye = lax.ppermute(y_even, 'gy', swaps['gy'][0])  3.27 us
    pallas_call x1, Pallas kernels, on_device(): pl.pallas_call(early_kernel, out_shape=(jax.ShapeDtypeStruct((len(EARLY),...  3 us
    ppermute x1, starting transfers between devices, on_device(): ce = lax.ppermute(c_even, 'gy', swaps['gy'][0])  2.19 us
  transfers between devices with their start and end apart: 7, of which 2 were waited for; matrix products, arithmetic and copies ran while one was open for 0% of the time, Pallas kernels for 16%

profile of v4, /device:TPU:1, one launch (start us, length us, event | category | flops | bytes accessed | tf_op | source)
XLA Modules:
  0.0 67.5 jit_solution(13984217852256914316)
XLA Ops:
  0.7 0.1 stack.27
  0.8 2.2 %pack.1 = (f32[4,32,8,128]{3,2,1,0:T(8,128)S(1)}, f32[4,32,8,128]{3,2,1,0:T(8,128)S(1)}, f32[4,8,32,128]{3,2,1,0:T(8,128)S(1)}, f32[4,8,32,128]{3,2,1,0:T(8,128)S(1)}) custom-call(s32[6]{0:T(128)S(1)} %convert_element_type.3.place_ref, f32[32,32,128]{2,1,0:T(8,128)} %start_hbm.1, f32[3,32,32,128]{3,2,1,0:T(8,128)} %vel_hbm.1), custom_call_target="tpu_custom_call" | custom-call | tf_op jit(solution)/shard_map/pack/pallas_call | solution.py:425
  2.9 3.3 %collective-permute-start.2 = (f32[4,8,32,128]{3,2,1,0:T(8,128)S(1)}, f32[4,8,32,128]{3,2,1,0:T(8,128)S(1)}, u32[]{:S(2)}, u32[]{:S(2)}) collective-permute-start(f32[4,8,32,128]{3,2,1,0:T(8,128)S(1)} %get-tuple-element.41), channel_id=1, source_target_pairs={{0,32},{32,0},{64,96},{96,64},{128,160},{160,128},{192,224},{224,1... | collective-permute-start | bytes 1572872 | tf_op jit(solution)/shard_map/ppermute | solution.py:435
  6.3 1.9 %collective-permute-start.3 = (f32[4,8,32,128]{3,2,1,0:T(8,128)S(1)}, f32[4,8,32,128]{3,2,1,0:T(8,128)S(1)}, u32[]{:S(2)}, u32[]{:S(2)}) collective-permute-start(f32[4,8,32,128]{3,2,1,0:T(8,128)S(1)} %get-tuple-element.42), channel_id=1, source_target_pairs={{32,64},{64,32},{96,128},{128,96},{160,192},{192,160},{33,65},{65,... | collective-permute-start | bytes 1572872 | tf_op jit(solution)/shard_map/ppermute | solution.py:434
  8.2 0.7 %collective-permute-start = (f32[4,32,8,128]{3,2,1,0:T(8,128)S(1)}, f32[4,32,8,128]{3,2,1,0:T(8,128)S(1)}, u32[]{:S(2)}, u32[]{:S(2)}) collective-permute-start(f32[4,32,8,128]{3,2,1,0:T(8,128)S(1)} %get-tuple-element.39), channel_id=1, source_target_pairs={{1,2},{2,1},{3,4},{4,3},{5,6},{6,5},{7,8},{8,7},{9,10},{10,9},{11,... | collective-permute-start | bytes 1572872 | tf_op jit(solution)/shard_map/ppermute | solution.py:436
  8.9 0.0 copy-start.2
  8.9 3.3 %collective-permute-start.1 = (f32[4,32,8,128]{3,2,1,0:T(8,128)S(1)}, f32[4,32,8,128]{3,2,1,0:T(8,128)S(1)}, u32[]{:S(2)}, u32[]{:S(2)}) collective-permute-start(f32[4,32,8,128]{3,2,1,0:T(8,128)S(1)} %get-tuple-element.40), channel_id=1, source_target_pairs={{0,1},{1,0},{2,3},{3,2},{4,5},{5,4},{6,7},{7,6},{8,9},{9,8},{10,11... | collective-permute-start | bytes 1572872 | tf_op jit(solution)/shard_map/ppermute | solution.py:437
  12.2 3.0 %early.1 = (f32[45,8,128]{2,1,0:T(8,128)S(1)}, f32[8,32,32,128]{3,2,1,0:T(8,128)S(1)}, f32[48,48,128]{2,1,0:T(8,128)S(1)}, f32[3,48,32,128]{3,2,1,0:T(8,128)S(1)}) custom-call(f32[8,32,32,128]{3,2,1,0:T(8,128)} %prior_hbm.1, f32[32,32,128]{2,1,0:T(8,128)} %start_hbm.1, f32[3,32,32,128]{3,2,1,0:T(8,128)} %vel_hbm.1), custom_call_target="tpu_custom_call" | custom-call | tf_op jit(solution)/shard_map/early/pallas_call | solution.py:442
  15.2 0.0 collective-permute-done.2.xe_ref
  15.2 1.9 %collective-permute-done.3.xo_ref = f32[4,8,32,128]{3,2,1,0:T(8,128)S(1)} collective-permute-done((f32[4,8,32,128]{3,2,1,0:T(8,128)S(1)}, f32[4,8,32,128]{3,2,1,0:T(8,128)S(1)}, u32[]{:S(2)}, u32[]{:S(2)}) %collective-permute-start.3) | collective-permute-done | bytes 524320 | tf_op jit(solution)/shard_map/ppermute | solution.py:434
  17.1 0.6 corner.1
  17.7 0.7 collective-permute-start.4
  18.3 2.2 %collective-permute-start.5 = (f32[182,128]{1,0:T(8,128)S(1)}, f32[182,128]{1,0:T(8,128)S(1)}, u32[]{:S(2)}, u32[]{:S(2)}) collective-permute-start(f32[182,128]{1,0:T(8,128)S(1)} %get-tuple-element.47), channel_id=1, source_target_pairs={{0,1},{1,0},{2,3},{3,2},{4,5},{5,4},{6,7},{7,6},{8,9},{9,8},{10,11... | collective-permute-start | bytes 279560 | tf_op jit(solution)/shard_map/ppermute | solution.py:466
  20.5 0.0 copy-done.2
  20.5 7.1 %inner.1 = (f32[48,48,128]{2,1,0:T(8,128)S(1)}, f32[48,48,128]{2,1,0:T(8,128)S(1)}, f32[48,48,128]{2,1,0:T(8,128)S(1)}, f32[48,48,128]{2,1,0:T(8,128)S(1)}, f32[...) custom-call(f32[8]{0:T(128)S(1)} %copy-done.2, ...), custom_call_target="tpu_custom_call", output_to_operand_aliasing={{0}: (6, {}), {9}: (7, {})} | custom-call | tf_op jit(solution)/shard_map/inner/pallas_call | solution.py:467
  27.6 0.0 collective-permute-done.yo_ref
  27.6 0.0 collective-permute-done.1.ye_ref
  27.7 0.0 collective-permute-done.4.co_ref
  27.7 0.0 collective-permute-done.5.ce_ref
  27.7 0.0 copy-start
  27.7 0.0 copy-start.1
  27.7 5.7 %outer.1 = (f32[4,48,16,128]{3,2,1,0:T(8,128)S(1)}, f32[4,48,16,128]{3,2,1,0:T(8,128)S(1)}, f32[48,48,128]{2,1,0:T(8,128)S(1)}, f32[48,48,128]{2,1,0:T(8,128)S(1...) custom-call(f32[8]{0:T(128)S(1)} %copy-done.2, ...), custom_call_target="tpu_custom_call", output_to_operand_aliasing={{0}: (8, {}), {1}: (9, {}), {2}: (10, {}), {3}: (11, {}), {... | custom-call | tf_op jit(solution)/shard_map/outer/pallas_call | solution.py:477
  33.4 0.1 collective-permute-start.6
  33.5 1.2 %collective-permute-done.6 = f32[8,128]{1,0:T(8,128)S(1)} collective-permute-done((f32[8,128]{1,0:T(8,128)S(1)}, f32[8,128]{1,0:T(8,128)S(1)}, u32[]{:S(2)}, u32[]{:S(2)}) %collective-permute-start.6) | collective-permute-done | bytes 4128 | tf_op jit(solution)/shard_map/ppermute | solution.py:491
  34.7 25.7 %all_to_all.11 = f32[128,2,128]{2,1,0:T(2,128)S(1)} all-to-all(f32[128,2,128]{2,1,0:T(2,128)S(1)} %bitcast.10), channel_id=1, replica_groups={{0,1,2,3,4,5,6,7,8,9,10,11,12,13,14,15,16,17,18,19,20,21,22,23,24,25,26..., dimensions={0} | all-to-all | bytes 262144 | tf_op jit(solution)/shard_map/all_to_all | solution.py:495
  60.4 0.0 copy-done
  60.4 0.0 copy-done.1
  60.4 7.0 %combine.1 = (f32[9,32,32,128]{3,2,1,0:T(8,128)}, f32[9,17]{1,0:T(8,128)}) custom-call(f32[256,128]{1,0:T(8,128)S(1)} %bitcast.9, f32[128,256]{1,0:T(8,128)S(1)} %copy-done.1, f32[128,256]{1,0:T(8,128)S(1)} %copy-done, f32[8,32,32,128]{3,2,1,0:T(8,128)S(1)} %get-tuple-element.48.prior_ref, f32[48,48,128]{2,1,0:T(8,128)S(1)} %get-tuple-element.65.rest_0_, ...), custom_call_target="tpu_custom_call" | custom-call | tf_op jit(solution)/shard_map/combine/pallas_call | solution.py:498
  (3 shorter events, 0.0 us)
Async XLA Ops:
  2.9 12.2 %collective-permute-start.2 = (f32[4,8,32,128]{3,2,1,0:T(8,128)S(1)}, f32[4,8,32,128]{3,2,1,0:T(8,128)S(1)}, u32[]{:S(2)}, u32[]{:S(2)}) collective-permute-start(f32[4,8,32,128]{3,2,1,0:T(8,128)S(1)} %get-tuple-element.41), channel_id=1, source_target_pairs={{0,32},{32,0},{64,96},{96,64},{128,160},{160,128},{192,224},{224,1... | collective-permute-start | bytes 1572872 | tf_op jit(solution)/shard_map/ppermute | solution.py:435
  6.3 10.8 %collective-permute-start.3 = (f32[4,8,32,128]{3,2,1,0:T(8,128)S(1)}, f32[4,8,32,128]{3,2,1,0:T(8,128)S(1)}, u32[]{:S(2)}, u32[]{:S(2)}) collective-permute-start(f32[4,8,32,128]{3,2,1,0:T(8,128)S(1)} %get-tuple-element.42), channel_id=1, source_target_pairs={{32,64},{64,32},{96,128},{128,96},{160,192},{192,160},{33,65},{65,... | collective-permute-start | bytes 1572872 | tf_op jit(solution)/shard_map/ppermute | solution.py:434
  8.2 19.4 %collective-permute-start = (f32[4,32,8,128]{3,2,1,0:T(8,128)S(1)}, f32[4,32,8,128]{3,2,1,0:T(8,128)S(1)}, u32[]{:S(2)}, u32[]{:S(2)}) collective-permute-start(f32[4,32,8,128]{3,2,1,0:T(8,128)S(1)} %get-tuple-element.39), channel_id=1, source_target_pairs={{1,2},{2,1},{3,4},{4,3},{5,6},{6,5},{7,8},{8,7},{9,10},{10,9},{11,... | collective-permute-start | bytes 1572872 | tf_op jit(solution)/shard_map/ppermute | solution.py:436
  8.9 11.6 %copy-start.2 = (f32[8]{0:T(128)S(1)}, f32[8]{0:T(128)}, u32[]{:S(2)}) copy-start(f32[8]{0:T(128)} %shifts_ref.3) | copy-start | bytes 100
  8.9 18.7 %collective-permute-start.1 = (f32[4,32,8,128]{3,2,1,0:T(8,128)S(1)}, f32[4,32,8,128]{3,2,1,0:T(8,128)S(1)}, u32[]{:S(2)}, u32[]{:S(2)}) collective-permute-start(f32[4,32,8,128]{3,2,1,0:T(8,128)S(1)} %get-tuple-element.40), channel_id=1, source_target_pairs={{0,1},{1,0},{2,3},{3,2},{4,5},{5,4},{6,7},{7,6},{8,9},{9,8},{10,11... | collective-permute-start | bytes 1572872 | tf_op jit(solution)/shard_map/ppermute | solution.py:437
  17.7 10.0 %collective-permute-start.4 = (f32[182,128]{1,0:T(8,128)S(1)}, f32[182,128]{1,0:T(8,128)S(1)}, u32[]{:S(2)}, u32[]{:S(2)}) collective-permute-start(f32[182,128]{1,0:T(8,128)S(1)} %get-tuple-element.46), channel_id=1, source_target_pairs={{1,2},{2,1},{3,4},{4,3},{5,6},{6,5},{7,8},{8,7},{9,10},{10,9},{11,... | collective-permute-start | bytes 279560 | tf_op jit(solution)/shard_map/ppermute | solution.py:465
  18.3 9.3 %collective-permute-start.5 = (f32[182,128]{1,0:T(8,128)S(1)}, f32[182,128]{1,0:T(8,128)S(1)}, u32[]{:S(2)}, u32[]{:S(2)}) collective-permute-start(f32[182,128]{1,0:T(8,128)S(1)} %get-tuple-element.47), channel_id=1, source_target_pairs={{0,1},{1,0},{2,3},{3,2},{4,5},{5,4},{6,7},{7,6},{8,9},{9,8},{10,11... | collective-permute-start | bytes 279560 | tf_op jit(solution)/shard_map/ppermute | solution.py:466
  27.7 32.7 %copy-start = (f32[128,256]{1,0:T(8,128)S(1)}, f32[128,256]{1,0:T(8,128)}, u32[]{:S(2)}) copy-start(f32[128,256]{1,0:T(8,128)} %constant.37.clone.second_ref) | copy-start | bytes 393220
  27.7 32.7 %copy-start.1 = (f32[128,256]{1,0:T(8,128)S(1)}, f32[128,256]{1,0:T(8,128)}, u32[]{:S(2)}) copy-start(f32[128,256]{1,0:T(8,128)} %constant.36.clone.first_ref) | copy-start | bytes 393220
  33.4 1.3 %collective-permute-start.6 = (f32[8,128]{1,0:T(8,128)S(1)}, f32[8,128]{1,0:T(8,128)S(1)}, u32[]{:S(2)}, u32[]{:S(2)}) collective-permute-start(f32[8,128]{1,0:T(8,128)S(1)} %get-tuple-element.64), channel_id=1, source_target_pairs={{0,32},{32,0},{64,96},{96,64},{128,160},{160,128},{192,224},{224,1... | collective-permute-start | bytes 12296 | tf_op jit(solution)/shard_map/ppermute | solution.py:491

commit v5 on v4

--- a/solution.py
+++ b/solution.py
@@ -77,8 +77,8 @@
 
     def put(at, f, row, n, low):
         for_low, for_high = (xe_ref, xo_ref) if low else (xo_ref, xe_ref)
-        last = jnp.where(odd_x, for_low[f, row, wy - n :, :], for_high[f, row, wy - n :, :])
-        first = jnp.where(odd_x, for_low[f, row, :n, :], for_high[f, row, :n, :])
+        last = jnp.where(odd_x, for_low[f, row, wy - 8 :, :], for_high[f, row, wy - 8 :, :])[8 - n :]
+        first = jnp.where(odd_x, for_low[f, row, :8, :], for_high[f, row, :8, :])[:n]
         even_ref[at : at + n, :] = jnp.where(odd_y, first, last)
         odd_ref[at : at + n, :] = jnp.where(odd_y, last, first)
 
@@ -418,7 +418,7 @@
     limit = pltpu.CompilerParams(vmem_limit_bytes=12 * 1024 * 1024)
     edge_y = jax.ShapeDtypeStruct((4, wx, H, wz), f32)
     edge_x = jax.ShapeDtypeStruct((4, H, wy, wz), f32)
-    corner = jax.ShapeDtypeStruct((CORNER, wz), f32)
+    corner = jax.ShapeDtypeStruct((CORNER + 10, wz), f32)
     start_hbm, velocity_hbm, prior_hbm = (
         pltpu.with_memory_space_constraint(v, pltpu.HBM) for v in (start, velocity, prior)
     )

time: 67.7 us -> 67.7 us (level)
  no operation moved by 1% of the time
where the time goes in v5:
time: 67.7 us; the launch traced here: 67.5 us
  blocking collectives  25.8 us (38%)
  Pallas kernels  25.4 us (38%)
  starting transfers between devices  12.1 us (18%)
  waiting for transfers between devices  3.03 us (4%)
  between operations  0.96 us (1%)
    all_to_all x1, blocking collectives, on_device(): lax.all_to_all(sums, AXES, 0, 0, tiled=True, axis_index_groups=cores)  25.8 us
    pallas_call x1, Pallas kernels, on_device(): pl.pallas_call(inner_kernel, out_shape=(*[field] * NEW, flow, strip, stri...  7.08 us
    pallas_call x1, Pallas kernels, on_device(): pl.pallas_call(functools.partial(combine_kernel, float(devices * wx * wy...  6.96 us
    pallas_call x1, Pallas kernels, on_device(): pl.pallas_call(outer_kernel, out_shape=(strip, strip, *[field] * NEW, jax...  5.6 us
    ppermute x1, starting transfers between devices, on_device(): xe = lax.ppermute(x_even, 'gx', swaps['gx'][0])  3.33 us
    ppermute x1, starting transfers between devices, on_device(): ye = lax.ppermute(y_even, 'gy', swaps['gy'][0])  3.27 us
    pallas_call x1, Pallas kernels, on_device(): pl.pallas_call(early_kernel, out_shape=(jax.ShapeDtypeStruct((len(EARLY),...  3 us
    ppermute x1, starting transfers between devices, on_device(): ce = lax.ppermute(c_even, 'gy', swaps['gy'][0])  2.19 us
  transfers between devices with their start and end apart: 7, of which 2 were waited for; matrix products, arithmetic and copies ran while one was open for 0% of the time, Pallas kernels for 16%

profile of v5, /device:TPU:1, one launch (start us, length us, event | category | flops | bytes accessed | tf_op | source)
XLA Modules:
  0.0 67.5 jit_solution(11036814289209864833)
XLA Ops:
  0.7 0.1 stack.27
  0.8 2.2 %pack.1 = (f32[4,32,8,128]{3,2,1,0:T(8,128)S(1)}, f32[4,32,8,128]{3,2,1,0:T(8,128)S(1)}, f32[4,8,32,128]{3,2,1,0:T(8,128)S(1)}, f32[4,8,32,128]{3,2,1,0:T(8,128)S(1)}) custom-call(s32[6]{0:T(128)S(1)} %convert_element_type.3.place_ref, f32[32,32,128]{2,1,0:T(8,128)} %start_hbm.1, f32[3,32,32,128]{3,2,1,0:T(8,128)} %vel_hbm.1), custom_call_target="tpu_custom_call" | custom-call | tf_op jit(solution)/shard_map/pack/pallas_call | solution.py:425
  2.9 3.3 %collective-permute-start.2 = (f32[4,8,32,128]{3,2,1,0:T(8,128)S(1)}, f32[4,8,32,128]{3,2,1,0:T(8,128)S(1)}, u32[]{:S(2)}, u32[]{:S(2)}) collective-permute-start(f32[4,8,32,128]{3,2,1,0:T(8,128)S(1)} %get-tuple-element.41), channel_id=1, source_target_pairs={{0,32},{32,0},{64,96},{96,64},{128,160},{160,128},{192,224},{224,1... | collective-permute-start | bytes 1572872 | tf_op jit(solution)/shard_map/ppermute | solution.py:435
  6.3 1.9 %collective-permute-start.3 = (f32[4,8,32,128]{3,2,1,0:T(8,128)S(1)}, f32[4,8,32,128]{3,2,1,0:T(8,128)S(1)}, u32[]{:S(2)}, u32[]{:S(2)}) collective-permute-start(f32[4,8,32,128]{3,2,1,0:T(8,128)S(1)} %get-tuple-element.42), channel_id=1, source_target_pairs={{32,64},{64,32},{96,128},{128,96},{160,192},{192,160},{33,65},{65,... | collective-permute-start | bytes 1572872 | tf_op jit(solution)/shard_map/ppermute | solution.py:434
  8.2 0.7 %collective-permute-start = (f32[4,32,8,128]{3,2,1,0:T(8,128)S(1)}, f32[4,32,8,128]{3,2,1,0:T(8,128)S(1)}, u32[]{:S(2)}, u32[]{:S(2)}) collective-permute-start(f32[4,32,8,128]{3,2,1,0:T(8,128)S(1)} %get-tuple-element.39), channel_id=1, source_target_pairs={{1,2},{2,1},{3,4},{4,3},{5,6},{6,5},{7,8},{8,7},{9,10},{10,9},{11,... | collective-permute-start | bytes 1572872 | tf_op jit(solution)/shard_map/ppermute | solution.py:436
  8.9 0.0 copy-start.2
  8.9 3.3 %collective-permute-start.1 = (f32[4,32,8,128]{3,2,1,0:T(8,128)S(1)}, f32[4,32,8,128]{3,2,1,0:T(8,128)S(1)}, u32[]{:S(2)}, u32[]{:S(2)}) collective-permute-start(f32[4,32,8,128]{3,2,1,0:T(8,128)S(1)} %get-tuple-element.40), channel_id=1, source_target_pairs={{0,1},{1,0},{2,3},{3,2},{4,5},{5,4},{6,7},{7,6},{8,9},{9,8},{10,11... | collective-permute-start | bytes 1572872 | tf_op jit(solution)/shard_map/ppermute | solution.py:437
  12.2 3.0 %early.1 = (f32[45,8,128]{2,1,0:T(8,128)S(1)}, f32[8,32,32,128]{3,2,1,0:T(8,128)S(1)}, f32[48,48,128]{2,1,0:T(8,128)S(1)}, f32[3,48,32,128]{3,2,1,0:T(8,128)S(1)}) custom-call(f32[8,32,32,128]{3,2,1,0:T(8,128)} %prior_hbm.1, f32[32,32,128]{2,1,0:T(8,128)} %start_hbm.1, f32[3,32,32,128]{3,2,1,0:T(8,128)} %vel_hbm.1), custom_call_target="tpu_custom_call" | custom-call | tf_op jit(solution)/shard_map/early/pallas_call | solution.py:442
  15.2 0.0 collective-permute-done.2.xe_ref
  15.2 1.9 %collective-permute-done.3.xo_ref = f32[4,8,32,128]{3,2,1,0:T(8,128)S(1)} collective-permute-done((f32[4,8,32,128]{3,2,1,0:T(8,128)S(1)}, f32[4,8,32,128]{3,2,1,0:T(8,128)S(1)}, u32[]{:S(2)}, u32[]{:S(2)}) %collective-permute-start.3) | collective-permute-done | bytes 524320 | tf_op jit(solution)/shard_map/ppermute | solution.py:434
  17.1 0.6 corner.1
  17.7 0.7 collective-permute-start.4
  18.3 2.2 %collective-permute-start.5 = (f32[192,128]{1,0:T(8,128)S(1)}, f32[192,128]{1,0:T(8,128)S(1)}, u32[]{:S(2)}, u32[]{:S(2)}) collective-permute-start(f32[192,128]{1,0:T(8,128)S(1)} %get-tuple-element.47), channel_id=1, source_target_pairs={{0,1},{1,0},{2,3},{3,2},{4,5},{5,4},{6,7},{7,6},{8,9},{9,8},{10,11... | collective-permute-start | bytes 294920 | tf_op jit(solution)/shard_map/ppermute | solution.py:466
  20.5 0.0 copy-done.2
  20.5 7.1 %inner.1 = (f32[48,48,128]{2,1,0:T(8,128)S(1)}, f32[48,48,128]{2,1,0:T(8,128)S(1)}, f32[48,48,128]{2,1,0:T(8,128)S(1)}, f32[48,48,128]{2,1,0:T(8,128)S(1)}, f32[...) custom-call(f32[8]{0:T(128)S(1)} %copy-done.2, ...), custom_call_target="tpu_custom_call", output_to_operand_aliasing={{0}: (6, {}), {9}: (7, {})} | custom-call | tf_op jit(solution)/shard_map/inner/pallas_call | solution.py:467
  27.6 0.0 collective-permute-done.yo_ref
  27.6 0.0 collective-permute-done.1.ye_ref
  27.6 0.0 collective-permute-done.4.co_ref
  27.6 0.0 collective-permute-done.5.ce_ref
  27.6 0.0 copy-start
  27.7 0.0 copy-start.1
  27.7 5.6 %outer.1 = (f32[4,48,16,128]{3,2,1,0:T(8,128)S(1)}, f32[4,48,16,128]{3,2,1,0:T(8,128)S(1)}, f32[48,48,128]{2,1,0:T(8,128)S(1)}, f32[48,48,128]{2,1,0:T(8,128)S(1...) custom-call(f32[8]{0:T(128)S(1)} %copy-done.2, ...), custom_call_target="tpu_custom_call", output_to_operand_aliasing={{0}: (8, {}), {1}: (9, {}), {2}: (10, {}), {3}: (11, {}), {... | custom-call | tf_op jit(solution)/shard_map/outer/pallas_call | solution.py:477
  33.3 0.1 collective-permute-start.6
  33.4 1.2 %collective-permute-done.6 = f32[8,128]{1,0:T(8,128)S(1)} collective-permute-done((f32[8,128]{1,0:T(8,128)S(1)}, f32[8,128]{1,0:T(8,128)S(1)}, u32[]{:S(2)}, u32[]{:S(2)}) %collective-permute-start.6) | collective-permute-done | bytes 4128 | tf_op jit(solution)/shard_map/ppermute | solution.py:491
  34.6 25.8 %all_to_all.11 = f32[128,2,128]{2,1,0:T(2,128)S(1)} all-to-all(f32[128,2,128]{2,1,0:T(2,128)S(1)} %bitcast.10), channel_id=1, replica_groups={{0,1,2,3,4,5,6,7,8,9,10,11,12,13,14,15,16,17,18,19,20,21,22,23,24,25,26..., dimensions={0} | all-to-all | bytes 262144 | tf_op jit(solution)/shard_map/all_to_all | solution.py:495
  60.4 0.0 copy-done
  60.4 0.0 copy-done.1
  60.4 7.0 %combine.1 = (f32[9,32,32,128]{3,2,1,0:T(8,128)}, f32[9,17]{1,0:T(8,128)}) custom-call(f32[256,128]{1,0:T(8,128)S(1)} %bitcast.9, f32[128,256]{1,0:T(8,128)S(1)} %copy-done.1, f32[128,256]{1,0:T(8,128)S(1)} %copy-done, f32[8,32,32,128]{3,2,1,0:T(8,128)S(1)} %get-tuple-element.48.prior_ref, f32[48,48,128]{2,1,0:T(8,128)S(1)} %get-tuple-element.65.rest_0_, ...), custom_call_target="tpu_custom_call" | custom-call | tf_op jit(solution)/shard_map/combine/pallas_call | solution.py:498
  (3 shorter events, 0.0 us)
Async XLA Ops:
  2.9 12.2 %collective-permute-start.2 = (f32[4,8,32,128]{3,2,1,0:T(8,128)S(1)}, f32[4,8,32,128]{3,2,1,0:T(8,128)S(1)}, u32[]{:S(2)}, u32[]{:S(2)}) collective-permute-start(f32[4,8,32,128]{3,2,1,0:T(8,128)S(1)} %get-tuple-element.41), channel_id=1, source_target_pairs={{0,32},{32,0},{64,96},{96,64},{128,160},{160,128},{192,224},{224,1... | collective-permute-start | bytes 1572872 | tf_op jit(solution)/shard_map/ppermute | solution.py:435
  6.3 10.8 %collective-permute-start.3 = (f32[4,8,32,128]{3,2,1,0:T(8,128)S(1)}, f32[4,8,32,128]{3,2,1,0:T(8,128)S(1)}, u32[]{:S(2)}, u32[]{:S(2)}) collective-permute-start(f32[4,8,32,128]{3,2,1,0:T(8,128)S(1)} %get-tuple-element.42), channel_id=1, source_target_pairs={{32,64},{64,32},{96,128},{128,96},{160,192},{192,160},{33,65},{65,... | collective-permute-start | bytes 1572872 | tf_op jit(solution)/shard_map/ppermute | solution.py:434
  8.2 19.4 %collective-permute-start = (f32[4,32,8,128]{3,2,1,0:T(8,128)S(1)}, f32[4,32,8,128]{3,2,1,0:T(8,128)S(1)}, u32[]{:S(2)}, u32[]{:S(2)}) collective-permute-start(f32[4,32,8,128]{3,2,1,0:T(8,128)S(1)} %get-tuple-element.39), channel_id=1, source_target_pairs={{1,2},{2,1},{3,4},{4,3},{5,6},{6,5},{7,8},{8,7},{9,10},{10,9},{11,... | collective-permute-start | bytes 1572872 | tf_op jit(solution)/shard_map/ppermute | solution.py:436
  8.9 11.6 %copy-start.2 = (f32[8]{0:T(128)S(1)}, f32[8]{0:T(128)}, u32[]{:S(2)}) copy-start(f32[8]{0:T(128)} %shifts_ref.3) | copy-start | bytes 100
  8.9 18.7 %collective-permute-start.1 = (f32[4,32,8,128]{3,2,1,0:T(8,128)S(1)}, f32[4,32,8,128]{3,2,1,0:T(8,128)S(1)}, u32[]{:S(2)}, u32[]{:S(2)}) collective-permute-start(f32[4,32,8,128]{3,2,1,0:T(8,128)S(1)} %get-tuple-element.40), channel_id=1, source_target_pairs={{0,1},{1,0},{2,3},{3,2},{4,5},{5,4},{6,7},{7,6},{8,9},{9,8},{10,11... | collective-permute-start | bytes 1572872 | tf_op jit(solution)/shard_map/ppermute | solution.py:437
  17.7 10.0 %collective-permute-start.4 = (f32[192,128]{1,0:T(8,128)S(1)}, f32[192,128]{1,0:T(8,128)S(1)}, u32[]{:S(2)}, u32[]{:S(2)}) collective-permute-start(f32[192,128]{1,0:T(8,128)S(1)} %get-tuple-element.46), channel_id=1, source_target_pairs={{1,2},{2,1},{3,4},{4,3},{5,6},{6,5},{7,8},{8,7},{9,10},{10,9},{11,... | collective-permute-start | bytes 294920 | tf_op jit(solution)/shard_map/ppermute | solution.py:465
  18.3 9.3 %collective-permute-start.5 = (f32[192,128]{1,0:T(8,128)S(1)}, f32[192,128]{1,0:T(8,128)S(1)}, u32[]{:S(2)}, u32[]{:S(2)}) collective-permute-start(f32[192,128]{1,0:T(8,128)S(1)} %get-tuple-element.47), channel_id=1, source_target_pairs={{0,1},{1,0},{2,3},{3,2},{4,5},{5,4},{6,7},{7,6},{8,9},{9,8},{10,11... | collective-permute-start | bytes 294920 | tf_op jit(solution)/shard_map/ppermute | solution.py:466
  27.6 32.7 %copy-start = (f32[128,256]{1,0:T(8,128)S(1)}, f32[128,256]{1,0:T(8,128)}, u32[]{:S(2)}) copy-start(f32[128,256]{1,0:T(8,128)} %constant.37.clone.second_ref) | copy-start | bytes 393220
  27.7 32.7 %copy-start.1 = (f32[128,256]{1,0:T(8,128)S(1)}, f32[128,256]{1,0:T(8,128)}, u32[]{:S(2)}) copy-start(f32[128,256]{1,0:T(8,128)} %constant.36.clone.first_ref) | copy-start | bytes 393220
  33.3 1.3 %collective-permute-start.6 = (f32[8,128]{1,0:T(8,128)S(1)}, f32[8,128]{1,0:T(8,128)S(1)}, u32[]{:S(2)}, u32[]{:S(2)}) collective-permute-start(f32[8,128]{1,0:T(8,128)S(1)} %get-tuple-element.64), channel_id=1, source_target_pairs={{0,32},{32,0},{64,96},{96,64},{128,160},{160,128},{192,224},{224,1... | collective-permute-start | bytes 12296 | tf_op jit(solution)/shard_map/ppermute | solution.py:491
